TPU v7x, 128 devices: a whole 4x4x4 slice. The times are simulated.
128 devices in a mesh: clip: 4 (over x), owner: 32 (over z, y, core).
Axes of the slice: x: 4, y: 4, z: 4, core: 2. Of those that a mesh axis runs over, the one named last changes fastest.
Arguments:
- mask_tiles: bfloat16 [2048, 16384], P('owner'), may hold values from 0 to 1
- correlation: int32 [256, 4], replicated, may hold values from 0 to 2047, as said below
- target: bfloat16 [256, 65536], P(('clip', 'owner')), may hold values from 0 to 1
- socs_kernels: float32 [2, 12, 15, 15], replicated, may hold values from -0.375 to 0.375
- socs_weights: float32 [12], replicated, may hold values from 0.2 to 1
Outputs:
- mask_grad: float32 [2048, 16384], P('owner', 'clip')
- clip_loss: float32 [256], P(('clip', 'owner'))
Inputs may be any that keep to these rules, and one draw needn't show every extreme that they name: `correlation`: tile t lies in row t // 64 and column t % 64 of the mask's tile grid and belongs to owner t // 64. Each clip's ids are the 2 x 2 neighbouring tiles at grid positions (r, c), (r, c+1), (r+1, c), (r+1, c+1), in that order, with r even. The clips of one device (aligned blocks of 2 clips) lie in distinct grid rows, so at most 2 of its 8 ids belong to one owner, and one pair of owners, the same for every block, gets exactly 2 from every block.
All inputs are finite; a program needn't handle non-finite values.
Results may differ from a plain program's by a relative error of at most 0.013.
Values may be sent and summed in bfloat16 or wider, within the bound.
A program may use at most 128 MiB of HBM per device.

v0:
```python
import math

import jax
import jax.numpy as jnp
from jax import lax
from jax.sharding import PartitionSpec as P

TS = 128
CAP = 2


steepness = 10.0
threshold = 0.3


def matmul(former, latter):
    return jnp.dot(former, latter, preferred_element_type=jnp.float32)


def dft_tables(extent):
    positions = jnp.arange(extent, dtype=jnp.int32)
    phases = positions[:, None] * positions[None, :] % extent
    angles = phases.astype(jnp.float32) * (2.0 * math.pi / extent)
    fwd_re = jnp.cos(angles).astype(jnp.bfloat16)
    fwd_im = (-jnp.sin(angles)).astype(jnp.bfloat16)
    inv_re = (jnp.cos(angles) / extent).astype(jnp.bfloat16)
    inv_im = (jnp.sin(angles) / extent).astype(jnp.bfloat16)
    return (fwd_re, fwd_im, inv_re, inv_im)


def kernel_spectra(socs_kernels, extent):
    kernel_span = socs_kernels.shape[-1]
    frequency = jnp.arange(extent, dtype=jnp.int32)
    offsets = jnp.arange(kernel_span, dtype=jnp.int32) - kernel_span // 2
    phases = frequency[:, None] * offsets[None, :] % extent
    angles = phases.astype(jnp.float32) * (2.0 * math.pi / extent)
    wave_re = jnp.cos(angles)
    wave_im = -jnp.sin(angles)
    highest = lax.Precision.HIGHEST
    ker_re = socs_kernels[0]
    ker_im = socs_kernels[1]
    mid_re = jnp.einsum("kab,vb->kav", ker_re, wave_re, precision=highest) - jnp.einsum(
        "kab,vb->kav", ker_im, wave_im, precision=highest
    )
    mid_im = jnp.einsum("kab,vb->kav", ker_re, wave_im, precision=highest) + jnp.einsum(
        "kab,vb->kav", ker_im, wave_re, precision=highest
    )
    spec_re = jnp.einsum("ua,kav->kuv", wave_re, mid_re, precision=highest) - jnp.einsum(
        "ua,kav->kuv", wave_im, mid_im, precision=highest
    )
    spec_im = jnp.einsum("ua,kav->kuv", wave_re, mid_im, precision=highest) + jnp.einsum(
        "ua,kav->kuv", wave_im, mid_re, precision=highest
    )
    return (spec_re, spec_im)


def clip_pass(window, target_row, spec_re, spec_im, socs_weights, tables, ambit):
    fwd_re, fwd_im, inv_re, inv_im = tables
    extent = window.shape[0]
    kernel_count = spec_re.shape[0]
    left_re = matmul(fwd_re, window).astype(jnp.bfloat16)
    left_im = matmul(fwd_im, window).astype(jnp.bfloat16)
    spec_real = matmul(left_re, fwd_re) - matmul(left_im, fwd_im)
    spec_imag = matmul(left_re, fwd_im) + matmul(left_im, fwd_re)
    intensity = jnp.zeros((extent, extent), jnp.float32)
    fields = []
    for kernel in range(kernel_count):
        prod_re = (spec_real * spec_re[kernel] - spec_imag * spec_im[kernel]).astype(jnp.bfloat16)
        prod_im = (spec_real * spec_im[kernel] + spec_imag * spec_re[kernel]).astype(jnp.bfloat16)
        half_re = (matmul(inv_re, prod_re) - matmul(inv_im, prod_im)).astype(jnp.bfloat16)
        half_im = (matmul(inv_re, prod_im) + matmul(inv_im, prod_re)).astype(jnp.bfloat16)
        field_re = matmul(half_re, inv_re) - matmul(half_im, inv_im)
        field_im = matmul(half_re, inv_im) + matmul(half_im, inv_re)
        scaled = socs_weights[kernel] / kernel_count
        intensity = intensity + scaled * (field_re * field_re + field_im * field_im)
        fields.append((field_re, field_im))
    resist = jax.nn.sigmoid(steepness * (intensity - threshold))
    positions = jnp.arange(extent, dtype=jnp.int32)
    inner = ((positions >= ambit) & (positions < extent - ambit)).astype(jnp.float32)
    interior = inner[:, None] * inner[None, :]
    mismatch = (resist - target_row.astype(jnp.float32).reshape(extent, extent)) * interior
    clip_error = jnp.sum(mismatch * mismatch) / float((extent - 2 * ambit) ** 2)
    sensitivity = 2.0 * mismatch * resist * (1.0 - resist) * steepness
    summed_re = jnp.zeros((extent, extent), jnp.float32)
    summed_im = jnp.zeros((extent, extent), jnp.float32)
    for kernel in range(kernel_count):
        field_re, field_im = fields[kernel]
        factor = sensitivity * (2.0 * socs_weights[kernel] / kernel_count)
        grad_re = (factor * field_re).astype(jnp.bfloat16)
        grad_im = (factor * field_im).astype(jnp.bfloat16)
        back_re = (matmul(fwd_re, grad_re) - matmul(fwd_im, grad_im)).astype(jnp.bfloat16)
        back_im = (matmul(fwd_re, grad_im) + matmul(fwd_im, grad_re)).astype(jnp.bfloat16)
        turn_re = matmul(back_re, fwd_re) - matmul(back_im, fwd_im)
        turn_im = matmul(back_re, fwd_im) + matmul(back_im, fwd_re)
        summed_re = summed_re + spec_re[kernel] * turn_re + spec_im[kernel] * turn_im
        summed_im = summed_im + spec_re[kernel] * turn_im - spec_im[kernel] * turn_re
    summed_re = summed_re.astype(jnp.bfloat16)
    summed_im = summed_im.astype(jnp.bfloat16)
    out_re = (matmul(inv_re, summed_re) - matmul(inv_im, summed_im)).astype(jnp.bfloat16)
    out_im = (matmul(inv_re, summed_im) + matmul(inv_im, summed_re)).astype(jnp.bfloat16)
    window_grad = matmul(out_re, inv_re) - matmul(out_im, inv_im)
    return (window_grad, clip_error)


def body(mask_tiles, correlation, target, socs_kernels, socs_weights):
    owners = lax.axis_size("owner")
    clips_axis = lax.axis_size("clip")
    clip_row = lax.axis_index("clip")
    owner_row = lax.axis_index("owner")
    tile_own = mask_tiles.shape[0]
    tile_pix = mask_tiles.shape[1]
    clip_dev = target.shape[0]
    references = 4 * clip_dev
    capacity = CAP
    slot_total = owners * capacity
    highest = lax.Precision.HIGHEST
    all_ids = correlation.reshape(clips_axis, owners, references)
    owner_of = all_ids // tile_own
    local_id = all_ids % tile_own
    positions = jnp.arange(references, dtype=jnp.int32)
    earlier = (owner_of[:, :, :, None] == owner_of[:, :, None, :]) & (
        positions[None, :] < positions[:, None]
    )[None, None]
    slot_rank = jnp.sum(earlier.astype(jnp.int32), axis=3)
    slot_of = owner_of * capacity + slot_rank
    slot_mine = slot_of[clip_row, owner_row]
    matches = (owner_of == owner_row)[..., None] & (
        slot_rank[..., None] == jnp.arange(capacity, dtype=jnp.int32)
    )
    slot_tile = jnp.sum(matches.astype(jnp.int32) * (local_id + 1)[..., None], axis=2) - 1
    slot_tile_row = slot_tile[clip_row]
    fetched = mask_tiles[jnp.maximum(slot_tile_row, 0)]
    outgoing = jnp.where(slot_tile_row[..., None] >= 0, fetched, jnp.zeros_like(fetched))
    incoming = lax.all_to_all(outgoing, "owner", split_axis=0, concat_axis=0, tiled=True)
    ref_tiles = incoming.reshape(slot_total, tile_pix)[slot_mine].reshape(clip_dev, 4, tile_pix)
    extent = 2 * TS
    ambit = socs_kernels.shape[-1] // 2
    tables = dft_tables(extent)
    spec_re, spec_im = kernel_spectra(socs_kernels, extent)

    def per_clip(clip_args):
        tile_rows, target_row = clip_args
        window = tile_rows.reshape(2, 2, TS, TS).transpose(0, 2, 1, 3).reshape(extent, extent)
        window_grad, clip_error = clip_pass(
            window, target_row, spec_re, spec_im, socs_weights, tables, ambit
        )
        split_grad = window_grad.reshape(2, TS, 2, TS).transpose(0, 2, 1, 3).reshape(4, TS * TS)
        return (split_grad, clip_error)

    pieces, losses = lax.map(per_clip, (ref_tiles, target))
    grads = pieces.reshape(references, tile_pix)
    placing = (slot_mine[:, None] == jnp.arange(slot_total, dtype=jnp.int32)[None, :]).astype(
        jnp.float32
    )
    tile_index = jnp.arange(tile_own, dtype=jnp.int32)
    out_slots = jnp.einsum("rs,rp->sp", placing, grads, precision=highest).reshape(
        owners, capacity, tile_pix
    )
    returned = lax.all_to_all(
        out_slots.astype(jnp.bfloat16), "owner", split_axis=0, concat_axis=0, tiled=True
    ).astype(out_slots.dtype)
    picking = (slot_tile_row.reshape(-1)[:, None] == tile_index[None, :]).astype(jnp.float32)
    tile_sums = jnp.einsum(
        "st,sp->tp", picking, returned.reshape(slot_total, tile_pix), precision=highest
    )
    mask_grad = lax.psum_scatter(
        tile_sums.astype(jnp.bfloat16), "clip", scatter_dimension=1, tiled=True
    ).astype(jnp.float32)
    return (mask_grad, losses)


def solution(mesh):
    placed = (P("owner", None), P(), P(("clip", "owner"), None), P(), P())
    return jax.shard_map(
        body,
        mesh=mesh,
        in_specs=placed,
        out_specs=(P("owner", "clip"), P(("clip", "owner"))),
        check_vma=False,
    )
```

profile of v0, /device:TPU:1, one launch (start us, length us, event | category | flops | bytes accessed | tf_op | source)
XLA Modules:
  0.0 720.0 jit_solution(11479434060641023851)
XLA Ops:
  9.2 3.2 gather_fusion
  12.4 3.2 reshape.300
  15.7 3.1 broadcast_select_fusion
  18.9 10.6 %all-to-all-start = ((bf16[32,2,16384]{2,1,0:T(2,128)(2,1)}), bf16[32,2,16384]{2,1,0:T(2,128)(2,1)}, u32[]{:S(2)}, u32[]{:S(2)}) async-start(bf16[32,2,16384]{2,1,0:T(2,128)(2,1)} %broadcast_select_fusion), calls=%async_computation | async-start | bytes 4194304 | tf_op jit(solution)/shard_map/all_to_all | solution.py:134
  47.0 2.8 fusion.1250
  49.8 4.4 add_bitcast_fusion
  56.7 3.8 fusion.1253
  60.5 4.6 subtract_bitcast_fusion
  65.2 3.5 copy.70
  69.4 4.1 reshape.291
  73.6 2.8 gather_fusion.1
  77.2 554.4 %while.17 = (s32[]{:T(128)}, f32[2,4,16384]{2,1,0:T(4,128)}, f32[2]{0:T(128)S(1)}, f32[12,256,256]{2,1,0:T(8,128)}, f32[]{:T(128)}, /*index=5*/bf16[2,4,16384]{2...) while((s32[]{:T(128)}, f32[2,4,16384]{2,1,0:T(4,128)}, ...), condition=%wide.region_4.5_spmd.clone.clone, body=%wide.region_2.4_spmd.clone.clone.sunk | while | flops 7087850496 | bytes 208540400 | solution.py:150
  217.2 5.2 multiply_reduce_fusion.2
  339.8 3.1 fusion.2324
  344.8 3.1 convolution_subtract_fusion.103
  492.5 5.2 multiply_reduce_fusion.2
  615.0 3.1 fusion.2324
  620.0 3.1 convolution_subtract_fusion.103
  635.1 3.5 copy.72
  638.6 7.6 %all-to-all-start.1 = ((bf16[32,2,16384]{2,1,0:T(2,128)(2,1)}), bf16[32,2,16384]{2,1,0:T(2,128)(2,1)}, u32[]{:S(2)}, u32[]{:S(2)}) async-start(bf16[32,2,16384]{2,1,0:T(2,128)(2,1)} %copy.72), calls=%async_computation.1 | async-start | bytes 4194304 | tf_op jit(solution)/shard_map/all_to_all | solution.py:159
  646.4 27.6 %all-to-all-done.1 = bf16[32,2,16384]{2,1,0:T(2,128)(2,1)} async-done(((bf16[32,2,16384]{2,1,0:T(2,128)(2,1)}), bf16[32,2,16384]{2,1,0:T(2,128)(2,1)}, u32[]{:S(2)}, u32[]{:S(2)}) %all-to-all-start.1) | async-done | bytes 2097184 | tf_op jit(solution)/shard_map/all_to_all | solution.py:159
  674.0 4.3 reshape.294
  678.3 3.8 convolution_convert_fusion.2
  682.1 28.7 %reduce-scatter.2.cloned.1.call-done = bf16[64,4096]{1,0:T(8,128)(2,1)} async-done(((bf16[64,16384]{1,0:T(8,128)(2,1)}), bf16[64,4096]{1,0:T(8,128)(2,1)}) %reduce-scatter.2.cloned.1.call-update) | async-done | bytes 524304 | tf_op jit(solution)/shard_map/reduce_scatter | solution.py:166
  (601 shorter events, 536.7 us)
Async XLA Ops:
  18.9 10.6 %copy-start.30 = (f32[2,12,15,15]{3,0,2,1:T(2,128)S(1)}, f32[2,12,15,15]{3,0,2,1:T(2,128)}, u32[]{:S(2)}) copy-start(f32[2,12,15,15]{3,0,2,1:T(2,128)} %param.10) | copy-start | bytes 64804
  18.9 11.7 %copy-start.31 = (f32[12]{0:T(128)S(1)}, f32[12]{0:T(128)}, u32[]{:S(2)}) copy-start(f32[12]{0:T(128)} %param.11) | copy-start | bytes 148
  18.9 50.6 %all-to-all-start = ((bf16[32,2,16384]{2,1,0:T(2,128)(2,1)}), bf16[32,2,16384]{2,1,0:T(2,128)(2,1)}, u32[]{:S(2)}, u32[]{:S(2)}) async-start(bf16[32,2,16384]{2,1,0:T(2,128)(2,1)} %broadcast_select_fusion), calls=%async_computation | async-start | bytes 4194304 | tf_op jit(solution)/shard_map/all_to_all | solution.py:134
  77.2 555.7 %copy-start.35 = (s32[8]{0:T(128)S(1)}, s32[8]{0:T(128)}, u32[]{:S(2)}) copy-start(s32[8]{0:T(128)} %copy-done.34) | copy-start | bytes 100
  77.2 555.7 %copy-start.36 = (s32[32,2]{0,1:T(2,128)S(1)}, s32[32,2]{0,1:T(2,128)}, u32[]{:S(2)}) copy-start(s32[32,2]{0,1:T(2,128)} %multiply_add_fusion) | copy-start | bytes 772
  206.5 8.1 %copy-start.27 = (bf16[2,65536]{1,0:T(2,128)(2,1)S(1)}, bf16[2,65536]{1,0:T(2,128)(2,1)}, u32[]{:S(2)}) copy-start(bf16[2,65536]{1,0:T(2,128)(2,1)} %get-tuple-element.2046) | copy-start | bytes 786436 | tf_op jit(solution)/shard_map/while
  227.6 6.2 copy-start.7
  227.6 6.2 copy-start.8
  227.6 6.2 copy-start.10
  227.6 6.2 copy-start.11
  227.6 6.2 copy-start.12
  227.6 6.2 copy-start.13
  227.6 6.2 copy-start.14
  227.7 6.2 copy-start.17
  227.7 6.2 copy-start.18
  481.6 8.3 %copy-start.27 = (bf16[2,65536]{1,0:T(2,128)(2,1)S(1)}, bf16[2,65536]{1,0:T(2,128)(2,1)}, u32[]{:S(2)}) copy-start(bf16[2,65536]{1,0:T(2,128)(2,1)} %get-tuple-element.2046) | copy-start | bytes 786436 | tf_op jit(solution)/shard_map/while
  502.8 6.0 copy-start.7
  502.8 6.0 copy-start.8
  502.8 6.0 copy-start.10
  631.6 7.0 copy-start.37
  638.6 7.6 %copy-start.33 = (s32[1,32,2]{1,2,0:T(2,128)S(1)}, s32[1,32,2]{1,2,0:T(2,128)}, u32[]{:S(2)}) copy-start(s32[1,32,2]{1,2,0:T(2,128)} %copy-done.32) | copy-start | bytes 772
  638.6 35.5 %all-to-all-start.1 = ((bf16[32,2,16384]{2,1,0:T(2,128)(2,1)}), bf16[32,2,16384]{2,1,0:T(2,128)(2,1)}, u32[]{:S(2)}, u32[]{:S(2)}) async-start(bf16[32,2,16384]{2,1,0:T(2,128)(2,1)} %copy.72), calls=%async_computation.1 | async-start | bytes 4194304 | tf_op jit(solution)/shard_map/all_to_all | solution.py:159
  646.1 64.6 %reduce-scatter.2.cloned.1.call-start = ((), (), s32[]{:S(2)}) async-start(), calls=%async_computation.3 | async-start | bytes 2621440 | tf_op jit(solution)/shard_map/reduce_scatter | solution.py:166
  674.0 38.8 %copy-start.1 = (bf16[64,16384]{1,0:T(8,128)(2,1)S(1)}, bf16[64,16384]{1,0:T(8,128)(2,1)}, u32[]{:S(2)}) copy-start(bf16[64,16384]{1,0:T(8,128)(2,1)} %param.7) | copy-start | bytes 6291460
  (44 other events, 230.8 us)
Sparse Core Ops, SparseCore 0:
  682.2 28.5 reduce-scatter.1
where the time goes:
time: 725 us; the launch traced here: 720 us
  matrix products  548 us (76%)
  waiting for transfers between devices  56.3 us (8%)
  local copies, waits for them, and re-layouts  43.9 us (6%)
  between operations  29.4 us (4%)
  starting transfers between devices  18.2 us (3%)
  other arithmetic  15.2 us (2%)
  loops' own time  9.33 us (1%)
    dot_general x404, matrix products, matmul(): return jnp.dot(former, latter, preferred_element_type=jnp.float32)  524 us
    reduce_scatter x1, waiting for transfers between devices, body(): lax.psum_scatter(tile_sums.astype(jnp.bfloat16), 'clip', scatter_dimensio...  28.7 us
    all_to_all x1, waiting for transfers between devices, body(): lax.all_to_all(out_slots.astype(jnp.bfloat16), 'owner', split_axis=0, con...  27.6 us
  transfers between devices with their start and end apart: 3, of which 2 were waited for; matrix products, arithmetic and copies ran while one was open for 4% of the time, Pallas kernels for 0%

commit v1 on v0

v1 whole, which is shorter than its diff:
```python
import functools

import jax
import jax.numpy as jnp
import ml_dtypes
import numpy as np
from jax import lax
from jax.experimental import pallas as pl
from jax.experimental.pallas import tpu as pltpu
from jax.sharding import PartitionSpec as P

TS=128; W=256; HF=128; KS=15; AM=7; NK=12; CH=24
f32=jnp.float32; bf16=jnp.bfloat16

def tables():
    u = np.arange(HF) + 0.5
    y = np.arange(W)
    ang = 2*np.pi*u[:,None]*y[None,:]/W
    R = np.concatenate([np.cos(ang), np.sin(ang)], 0)
    b = np.arange(KS)-AM
    ang2 = 2*np.pi*u[:,None]*b[None,:]/W
    T = np.concatenate([np.cos(ang2), np.sin(ang2)], 0)
    T16 = np.zeros((W,16)); T16[:,:KS]=T
    hi = T16.astype(np.float32).astype(ml_dtypes.bfloat16)
    lo = (T16-hi.astype(np.float64)).astype(np.float32).astype(ml_dtypes.bfloat16)
    T3 = np.concatenate([hi,hi,lo],1)
    TB = np.zeros((W, 128)); TB[:,:KS]=T
    TB = TB.T.astype(np.float32)
    Rb = R.astype(np.float32).astype(ml_dtypes.bfloat16)
    return Rb, np.ascontiguousarray(Rb.T), T3, TB

def dot(a,b):
    return jnp.dot(a,b,preferred_element_type=f32)

def gen_spectra(taps_ref, sw_ref, t3_ref, tb_ref, pad, mid, spec, level, su):
    pad[...] = jnp.zeros(pad.shape, f32)
    for c in range(CH):
        pad[c,:KS,:KS] = taps_ref[c]*jnp.sqrt(sw_ref[c % NK]*(1.0/NK))
    level[...] = jnp.broadcast_to(jnp.sum(jnp.sum(pad[...],axis=1,keepdims=True),axis=2,keepdims=True)*0.5,level.shape)
    m = jnp.dot(pad[...].reshape(CH*16,128), tb_ref[...], precision=lax.Precision.HIGHEST, preferred_element_type=f32).reshape(CH,16,W)
    hi = m.astype(bf16)
    lo = (m-hi.astype(f32)).astype(bf16)
    mid[:,0:16,:]=hi
    mid[:,16:32,:]=lo
    mid[:,32:48,:]=hi
    def body(c,_):
        q = dot(t3_ref[...], mid[c])
        cc=q[:HF,:HF]; cs=q[:HF,HF:]; sc=q[HF:,:HF]; ss=q[HF:,HF:]
        spec[c,0]=cc-ss; spec[c,1]=sc+cs; spec[c,2]=cc+ss; spec[c,3]=sc-cs
        return 0
    lax.fori_loop(0,CH,body,0,unroll=su)

def compute(n, window, target, spec, r_ref, rt_ref, sfreq, acc, field, inten, put, loss_ref, level, rsum_ref, fu, bu):
    R=r_ref[...]; RT=rt_ref[...]
    for i in range(n):
        x = window(i)
        t = (dot(R, x)-rsum_ref[...]).astype(bf16)
        s = dot(t, RT)*(0.5/(HF*HF))
        cc=s[:HF,:HF]; cs=s[:HF,HF:]; sc=s[HF:,:HF]; ss=s[HF:,HF:]
        sfreq[i,0]=cc-ss; sfreq[i,1]=sc+cs; sfreq[i,2]=cc+ss; sfreq[i,3]=sc-cs
        inten[i]=jnp.zeros((W,W),f32)
    def fwd(c,_):
        for i in range(n):
            p,q,p2,q2 = (sfreq[i,j] for j in range(4))
            m,nn,m2,n2 = (spec[c,j] for j in range(4))
            a=p*m-q*nn; b=p*nn+q*m; a2=p2*m2-q2*n2; b2=p2*n2+q2*m2
            P=jnp.concatenate([jnp.concatenate([a+a2,b-b2],1),jnp.concatenate([b+b2,a2-a],1)],0).astype(bf16)
            U=dot(P,r_ref[...]).astype(bf16)
            E=dot(rt_ref[...],U)+level[c]
            field[c,i]=E
            inten[i]=inten[i]+E*E
        return 0
    lax.fori_loop(0,CH,fwd,0,unroll=fu)
    row=lax.broadcasted_iota(jnp.int32,(W,W),0); col=lax.broadcasted_iota(jnp.int32,(W,W),1)
    inside=(row>=AM)&(row<W-AM)&(col>=AM)&(col<W-AM)
    for i in range(n):
        I=inten[i]
        Rs=1.0/(1.0+jnp.exp(-10.0*(I-0.3)))
        Z=jnp.where(inside,Rs-target(i).astype(f32),0.0)
        loss_ref[i]=jnp.sum(Z*Z)*(1.0/((W-2*AM)**2))
        inten[i]=40.0*Z*Rs*(1.0-Rs)
        acc[i]=jnp.zeros((4,HF,HF),f32)
    def bwd(c,_):
        for i in range(n):
            g=(inten[i]*field[c,i]).astype(bf16)
            V=dot(g,rt_ref[...]).astype(bf16)
            s=dot(r_ref[...],V)
            cc=s[:HF,:HF]; cs=s[:HF,HF:]; sc=s[HF:,:HF]; ss=s[HF:,HF:]
            p=cc-ss; q=sc+cs; p2=cc+ss; q2=sc-cs
            m,nn,m2,n2 = (spec[c,j] for j in range(4))
            acc[i,0]+=p*m+q*nn
            acc[i,1]+=q*m-p*nn
            acc[i,2]+=p2*m2+q2*n2
            acc[i,3]+=q2*m2-p2*n2
        return 0
    lax.fori_loop(0,CH,bwd,0,unroll=bu)
    for i in range(n):
        a,b,a2,b2=(acc[i,j] for j in range(4))
        P=(jnp.concatenate([jnp.concatenate([a+a2,b-b2],1),jnp.concatenate([b+b2,a2-a],1)],0)*(0.5/(HF*HF))).astype(bf16)
        U=dot(P,r_ref[...]).astype(bf16)
        put(i,dot(rt_ref[...],U))

def clip_kernel(su, fu, bu, idx_ref, sw_ref, tiles_ref, target_ref, taps_ref, r_ref, rt_ref, t3_ref, tb_ref, rsum_ref, grad_ref, loss_ref, pad, mid, spec, sfreq, acc, field, inten, level):
    gen_spectra(taps_ref, sw_ref, t3_ref, tb_ref, pad, mid, spec, level, su)
    def window(i):
        t=[tiles_ref[idx_ref[4*i+j]] for j in range(4)]
        return jnp.concatenate([jnp.concatenate(t[:2],1),jnp.concatenate(t[2:],1)],0)
    def put(i,d):
        d=d.astype(bf16)
        for j in range(4):
            r,c=divmod(j,2)
            grad_ref[4*i+j]=d[r*HF:(r+1)*HF,c*HF:(c+1)*HF]
    compute(2, window, lambda i: target_ref[i], spec, r_ref, rt_ref, sfreq, acc, field, inten, put, loss_ref, level, rsum_ref, fu, bu)


def clip_grads(idx, sw, tiles, target, taps):
    Rb,RTb,T3,TB=tables()
    V=pl.BlockSpec(memory_space=pltpu.VMEM); S=pl.BlockSpec(memory_space=pltpu.SMEM)
    rsum=np.broadcast_to(0.5*Rb.astype(np.float32).sum(1,keepdims=True),(W,W)).copy()
    return pl.pallas_call(functools.partial(clip_kernel,8,4,4),
        out_shape=(jax.ShapeDtypeStruct((8,TS,TS),bf16), jax.ShapeDtypeStruct((2,),f32)),
        in_specs=[S,S]+[V]*8, out_specs=(V,S),
        scratch_shapes=[pltpu.VMEM((CH,16,128),f32), pltpu.VMEM((CH,48,W),bf16), pltpu.VMEM((CH,4,HF,HF),f32),
            pltpu.VMEM((2,4,HF,HF),f32), pltpu.VMEM((2,4,HF,HF),f32), pltpu.VMEM((CH,2,W,W),f32), pltpu.VMEM((2,W,W),f32), pltpu.VMEM((CH,1,W),f32)],
        compiler_params=pltpu.CompilerParams(vmem_limit_bytes=56*2**20),
    )(idx, sw, tiles, target, taps, jnp.asarray(Rb), jnp.asarray(RTb), jnp.asarray(T3), jnp.asarray(TB), jnp.asarray(rsum))


def sum_kernel(first_ref, got_ref, out_ref, total):
    chip = lax.axis_index("owner") // 2
    total[...] = jnp.zeros(total.shape, f32)

    def step(s, _):
        for i in range(2):
            first = first_ref[2 * s + i]

            @pl.when(first // 128 == chip)
            def _():
                at = pl.multiple_of(first % 64 * 32, 32)
                total[pl.ds(at, 32), :] += got_ref[s, 0].astype(f32)
                total[pl.ds(at + 32, 32), :] += got_ref[s, 1].astype(f32)
        return 0

    lax.fori_loop(0, 128, step, 0)
    for t in range(8):
        for j in range(32):
            out_ref[8 * t : 8 * t + 8, 128 * j : 128 * j + 128] = total[pl.ds(256 * t + j, 8, stride=32), :]


def body(mask_tiles, correlation, target, socs_kernels, socs_weights):
    plane = lax.axis_index("clip")
    owner = lax.axis_index("owner")
    first = correlation[:, 0]
    near = lax.dynamic_slice(first, (plane * 64,), (64,)).reshape(32, 2)
    hit = near // 128 == owner // 2
    column = jnp.where(hit[:, 0], near[:, 0], near[:, 1]) % 64
    column = jnp.minimum(column, 62)
    outgoing = mask_tiles.reshape(64, TS, TS)[column[:, None] + jnp.arange(2)]
    incoming = lax.all_to_all(outgoing, "owner", split_axis=0, concat_axis=0, tiled=True).reshape(64, TS, TS)
    own = near[owner]
    idx = (own[:, None] // 128 * 4 + jnp.arange(4)).reshape(8)
    grads, losses = clip_grads(idx, socs_weights, incoming, target.reshape(2, W, W), socs_kernels.reshape(CH, KS, KS))
    which = (jnp.arange(16) == own[1] // 128).astype(jnp.int32)
    back = grads.reshape(2, 2, 2, 4, 32, TS)[which]
    back = back.transpose(3, 0, 1, 2, 4, 5).reshape(128, 2, 32, TS)
    got = lax.all_to_all(back, ("clip", "owner"), split_axis=0, concat_axis=0, tiled=True)
    V=pl.BlockSpec(memory_space=pltpu.VMEM); S=pl.BlockSpec(memory_space=pltpu.SMEM)
    mask_grad = pl.pallas_call(sum_kernel, out_shape=jax.ShapeDtypeStruct((64, 4096), f32),
        in_specs=[S, V], out_specs=V, scratch_shapes=[pltpu.VMEM((2048, 128), f32)],
    )(first, got)
    return mask_grad, losses


def solution(mesh):
    placed = (P("owner", None), P(), P(("clip", "owner"), None), P(), P())
    return jax.shard_map(body, mesh=mesh, in_specs=placed,
        out_specs=(P("owner", "clip"), P(("clip", "owner"))), check_vma=False)
```

time: 725 us -> 110 us (0.15)
  matrix products: 548 us -> 0 us
  blocking collectives: 0 us -> 37.4 us
  waiting for transfers between devices: 56.3 us -> 22.4 us
  local copies, waits for them, and re-layouts: 43.9 us -> 11.9 us
  between operations: 29.4 us -> 3.37 us
  Pallas kernels: 0 us -> 24.8 us
  other arithmetic: 15.2 us -> 0.39 us
  loops' own time: 9.33 us -> 0 us
  starting transfers between devices: 18.2 us -> 9.73 us
    dot_general x414 -> x0, matrix products: 548 us -> none  [the longest x404 524 us: matmul(): return jnp.dot(former, latter, preferred_element_type=jnp.float32)]
    all_to_all x0 -> x1, blocking collectives: none -> 37.4 us  [body(): lax.all_to_all(back, ('clip', 'owner'), split_axis=0, concat_axis=0, tile...]
    reduce_scatter x1 -> x0, waiting for transfers between devices: 28.7 us -> none  [body(): lax.psum_scatter(tile_sums.astype(jnp.bfloat16), 'clip', scatter_dimensio...]
    all_to_all x1 -> x0, waiting for transfers between devices: 27.6 us -> none  [body(): lax.all_to_all(out_slots.astype(jnp.bfloat16), 'owner', split_axis=0, con...]
    pallas_call x0 -> x2, Pallas kernels: none -> 24.8 us  [the longest x1 16.9 us: clip_grads(): pl.pallas_call(functools.partial(clip_kernel, 8, 4, 4), out_shape=(jax.Sh...]
    all_to_all x1, waiting for transfers between devices: 0.01 us -> 22.4 us  [body(): lax.all_to_all(outgoing, 'owner', split_axis=0, concat_axis=0, tiled=True)]
    reshape x8 -> x1, local copies, waits for them, and re-layouts: 12.7 us -> 0.1 us  [body(): near = lax.dynamic_slice(first, (plane * 64,), (64,)).reshape(32, 2)]
    convert_element_type x19 -> x0, other arithmetic: 11.1 us -> none  [the longest x2 2.96 us: clip_pass(): summed_im = summed_im.astype(jnp.bfloat16)]
  transfers between devices with their start and end apart: 3 -> 1, of which waited for: 2 -> 1; matrix products, arithmetic and copies ran while one was open for 4% -> 3% of each run, Pallas kernels for 0% -> 0%
where the time goes in v1:
time: 110 us
  blocking collectives  37.4 us (34%)
  Pallas kernels  24.8 us (23%)
  waiting for transfers between devices  22.4 us (20%)
  local copies, waits for them, and re-layouts  11.9 us (11%)
  starting transfers between devices  9.73 us (9%)
  between operations  3.37 us (3%)
    all_to_all x1, blocking collectives, body(): lax.all_to_all(back, ('clip', 'owner'), split_axis=0, concat_axis=0, tile...  37.4 us
    all_to_all x1, waiting for transfers between devices, body(): lax.all_to_all(outgoing, 'owner', split_axis=0, concat_axis=0, tiled=True)  22.4 us
    pallas_call x1, Pallas kernels, clip_grads(): pl.pallas_call(functools.partial(clip_kernel, 8, 4, 4), out_shape=(jax.Sh...  16.9 us
    all_to_all x1, starting transfers between devices, body(): lax.all_to_all(outgoing, 'owner', split_axis=0, concat_axis=0, tiled=True)  9.73 us
    pallas_call x1, Pallas kernels, body(): pl.pallas_call(sum_kernel, out_shape=jax.ShapeDtypeStruct((64, 4096), f32...  7.81 us
    unnamed x11, local copies, waits for them, and re-layouts  4.93 us
  transfers between devices with their start and end apart: 1, of which 1 were waited for; matrix products, arithmetic and copies ran while one was open for 3% of the time, Pallas kernels for 0%

profile of v1, /device:TPU:1, one launch (start us, length us, event | category | flops | bytes accessed | tf_op | source)
XLA Modules:
  0.0 109.9 jit_solution(5559896184893814685)
XLA Ops:
  0.6 0.7 slice.16
  1.3 0.1 dynamic-slice_reduce_fusion
  1.4 0.1 reshape.155
  1.6 2.2 %copy.15 = bf16[8,8,128,128]{3,2,1,0:T(8,128)(2,1)S(1)} copy(bf16[8,8,128,128]{3,1,2,0:T(8,128)(2,1)} %bitcast.34) | data formatting | bytes 4194304
  3.7 0.0 copy-done.3
  3.7 0.2 fusion.4
  3.9 0.1 compare_select_fusion
  4.0 0.1 reshape.164
  4.1 2.1 %gather_fusion = bf16[64,128,128]{2,1,0:T(8,128)(2,1)} fusion(bf16[64,128,128]{2,1,0:T(8,128)(2,1)S(1)} %bitcast.31, s32[1024]{0:T(1024)S(1)} %pad_clamp_fusion.1), kind=kCustom, calls=%fused_computation | custom fusion | bytes 4194560 | tf_op jit(solution)/shard_map/gather | solution.py:158
  6.3 9.7 %all-to-all-start = ((bf16[32,2,128,128]{3,2,1,0:T(8,128)(2,1)}), bf16[32,2,128,128]{3,2,1,0:T(8,128)(2,1)S(1)}, u32[]{:S(2)}, u32[]{:S(2)}) async-start(bf16[32,2,128,128]{3,2,1,0:T(8,128)(2,1)} %bitcast.30), calls=%async_computation | async-start | bytes 4194304 | tf_op jit(solution)/shard_map/all_to_all | solution.py:159
  16.1 0.6 slice.20
  18.6 0.1 iota_add_fusion
  18.7 0.7 add.89.idx_ref
  19.3 0.0 copy-done.1
  19.3 0.7 copy.18
  20.1 0.0 copy-done.2
  20.1 0.7 copy.13
  21.4 22.4 %all-to-all-done = bf16[32,2,128,128]{3,2,1,0:T(8,128)(2,1)S(1)} async-done(((bf16[32,2,128,128]{3,2,1,0:T(8,128)(2,1)}), bf16[32,2,128,128]{3,2,1,0:T(8,128)(2,1)S(1)}, u32[]{:S(2)}, u32[]{:S(2)}) %all-to-all-start) | async-done | bytes 2097184 | tf_op jit(solution)/shard_map/all_to_all | solution.py:159
  43.9 1.3 %copy-done = bf16[32,2,128,128]{3,2,1,0:T(8,128)(2,1)} copy-done((bf16[32,2,128,128]{3,2,1,0:T(8,128)(2,1)}, bf16[32,2,128,128]{3,2,1,0:T(8,128)(2,1)S(1)}, u32[]{:S(2)}) %copy-start) | copy-done | bytes 2097176
  45.2 16.9 %shard_map.113 = (bf16[8,128,128]{2,1,0:T(8,128)(2,1)}, f32[2]{0:T(128)}) custom-call(s32[8]{0:T(128)} %add.89.idx_ref, f32[12]{0:T(128)} %sw_ref.1, bf16[64,128,128]{2,1,0:T(8,128)(2,1)} %bitcast.29, bf16[2,256,256]{2,1,0:T(8,128)(2,1)} %bitcast.35, f32[24,15,15]{2,1,0:T(8,128)} %bitcast.36, bf16[256,256]{1,0:T(8,128)(2,1)} %constant.91.clone.r_ref, ...), custom_call_target="tpu_custom_call" | custom-call | tf_op jit(solution)/shard_map/pallas_call | solution.py:120
  62.2 1.9 %gather_fusion.1 = bf16[16,2,2,4,32,128]{5,4,3,2,1,0:T(8,128)(2,1)S(1)} fusion(bf16[2,2,2,4,32,128]{5,4,3,2,1,0:T(8,128)(2,1)} %bitcast.28, s32[1024]{0:T(1024)S(1)} %pad_clamp_fusion), kind=kCustom, calls=%fused_computation.1 | custom fusion | bytes 4194368 | tf_op jit(solution)/shard_map/gather | solution.py:164
  64.1 0.7 copy.14
  64.7 37.4 %all_to_all.10.got_ref = bf16[128,2,32,128]{3,2,1,0:T(8,128)(2,1)} all-to-all(bf16[128,2,32,128]{3,2,1,0:T(8,128)(2,1)S(1)} %bitcast.33), channel_id=1, replica_groups=mesh['clip'=4,'owner'=32] {'clip','owner'}, dimensions={0} | all-to-all | bytes 4194304 | tf_op jit(solution)/shard_map/all_to_all | solution.py:166
  102.1 7.8 %shard_map.114 = f32[64,4096]{1,0:T(8,128)} custom-call(s32[256]{0:T(256)} %bitcast.38, bf16[128,2,32,128]{3,2,1,0:T(8,128)(2,1)} %all_to_all.10.got_ref), custom_call_target="tpu_custom_call" | custom-call | tf_op jit(solution)/shard_map/pallas_call | solution.py:168
  (10 shorter events, 0.1 us)
Async XLA Ops:
  1.3 2.4 %copy-start.3 = (s32[256,1]{0,1:T(1,128)}, s32[256,1]{0,1:T(1,128)S(1)}, u32[]{:S(2)}) copy-start(s32[256,1]{0,1:T(1,128)S(1)} %slice.16) | copy-start | bytes 3076
  6.3 13.0 %copy-start.1 = (bf16[2,65536]{1,0:T(2,128)(2,1)S(1)}, bf16[2,65536]{1,0:T(2,128)(2,1)}, u32[]{:S(2)}) copy-start(bf16[2,65536]{1,0:T(2,128)(2,1)} %param.12) | copy-start | bytes 786436
  6.3 13.8 %copy-start.2 = (f32[2,12,15,15]{3,0,2,1:T(2,128)S(1)}, f32[2,12,15,15]{3,0,2,1:T(2,128)}, u32[]{:S(2)}) copy-start(f32[2,12,15,15]{3,0,2,1:T(2,128)} %param.13) | copy-start | bytes 64804
  6.3 37.6 %all-to-all-start = ((bf16[32,2,128,128]{3,2,1,0:T(8,128)(2,1)}), bf16[32,2,128,128]{3,2,1,0:T(8,128)(2,1)S(1)}, u32[]{:S(2)}, u32[]{:S(2)}) async-start(bf16[32,2,128,128]{3,2,1,0:T(8,128)(2,1)} %bitcast.30), calls=%async_computation | async-start | bytes 4194304 | tf_op jit(solution)/shard_map/all_to_all | solution.py:159
  43.9 1.3 %copy-start = (bf16[32,2,128,128]{3,2,1,0:T(8,128)(2,1)}, bf16[32,2,128,128]{3,2,1,0:T(8,128)(2,1)S(1)}, u32[]{:S(2)}) copy-start(bf16[32,2,128,128]{3,2,1,0:T(8,128)(2,1)S(1)} %all-to-all-done) | copy-start | bytes 6291460

commit v2 on v1

--- a/solution.py
+++ b/solution.py
@@ -10,6 +10,7 @@
 from jax.sharding import PartitionSpec as P
 
 TS=128; W=256; HF=128; KS=15; AM=7; NK=12; CH=24
+MESH = pl.DeviceIdType.MESH
 f32=jnp.float32; bf16=jnp.bfloat16
 
 def tables():
@@ -100,73 +101,140 @@
         U=dot(P,r_ref[...]).astype(bf16)
         put(i,dot(rt_ref[...],U))
 
-def clip_kernel(su, fu, bu, idx_ref, sw_ref, tiles_ref, target_ref, taps_ref, r_ref, rt_ref, t3_ref, tb_ref, rsum_ref, grad_ref, loss_ref, pad, mid, spec, sfreq, acc, field, inten, level):
-    gen_spectra(taps_ref, sw_ref, t3_ref, tb_ref, pad, mid, spec, level, su)
+
+def partner(k, plane, owner):
+    y = (owner // 2 + k // 2) % 4
+    z = (owner // 8 + k // 8) % 4
+    return (plane + k // 32) % 4, z * 8 + y * 2 + (owner + k) % 2
+
+
+def step_kernel(first, sw, mask, target, taps, r, rt, t3, tb, rsum, got, loss,
+        out, recv, back, grads, pad, mid, spec, sfreq, acc, field, inten, level, fs, fr, bs, br, ls):
+    plane = lax.axis_index("clip")
+    owner = lax.axis_index("owner")
+    me = plane * 32 + owner
+    chip = owner // 2
+    barrier = pltpu.get_barrier_semaphore()
+
+    def greet(k, _):
+        pl.semaphore_signal(barrier, inc=1, device_id=partner(k, plane, owner), device_id_type=MESH)
+        return 0
+
+    lax.fori_loop(1, 128, greet, 0)
+
+    def pick(d, _):
+        near = first[plane * 64 + 2 * d]
+        far = first[plane * 64 + 2 * d + 1]
+        column = jnp.minimum(lax.rem(jnp.where(near // 128 == chip, near, far), 64), 62)
+        out[d, 0] = mask[column]
+        out[d, 1] = mask[column + 1]
+        return 0
+
+    lax.fori_loop(0, 32, pick, 0)
+    pl.semaphore_wait(barrier, 127)
+
+    def fetch(k, _):
+        _, to = partner(k, plane, owner)
+        pltpu.make_async_remote_copy(src_ref=out.at[to], dst_ref=recv.at[owner], send_sem=fs, recv_sem=fr,
+            device_id=(plane, to), device_id_type=MESH).start()
+        return 0
+
+    lax.fori_loop(1, 32, fetch, 0)
+    recv[owner] = out[owner]
+    gen_spectra(taps, sw, t3, tb, pad, mid, spec, level, 8)
+    pltpu.make_async_copy(recv.at[pl.ds(0, 31)], recv.at[pl.ds(0, 31)], fr).wait()
+
     def window(i):
-        t=[tiles_ref[idx_ref[4*i+j]] for j in range(4)]
-        return jnp.concatenate([jnp.concatenate(t[:2],1),jnp.concatenate(t[2:],1)],0)
-    def put(i,d):
-        d=d.astype(bf16)
-        for j in range(4):
-            r,c=divmod(j,2)
-            grad_ref[4*i+j]=d[r*HF:(r+1)*HF,c*HF:(c+1)*HF]
-    compute(2, window, lambda i: target_ref[i], spec, r_ref, rt_ref, sfreq, acc, field, inten, put, loss_ref, level, rsum_ref, fu, bu)
-
-
-def clip_grads(idx, sw, tiles, target, taps):
-    Rb,RTb,T3,TB=tables()
-    V=pl.BlockSpec(memory_space=pltpu.VMEM); S=pl.BlockSpec(memory_space=pltpu.SMEM)
-    rsum=np.broadcast_to(0.5*Rb.astype(np.float32).sum(1,keepdims=True),(W,W)).copy()
-    return pl.pallas_call(functools.partial(clip_kernel,8,4,4),
-        out_shape=(jax.ShapeDtypeStruct((8,TS,TS),bf16), jax.ShapeDtypeStruct((2,),f32)),
-        in_specs=[S,S]+[V]*8, out_specs=(V,S),
-        scratch_shapes=[pltpu.VMEM((CH,16,128),f32), pltpu.VMEM((CH,48,W),bf16), pltpu.VMEM((CH,4,HF,HF),f32),
-            pltpu.VMEM((2,4,HF,HF),f32), pltpu.VMEM((2,4,HF,HF),f32), pltpu.VMEM((CH,2,W,W),f32), pltpu.VMEM((2,W,W),f32), pltpu.VMEM((CH,1,W),f32)],
-        compiler_params=pltpu.CompilerParams(vmem_limit_bytes=56*2**20),
-    )(idx, sw, tiles, target, taps, jnp.asarray(Rb), jnp.asarray(RTb), jnp.asarray(T3), jnp.asarray(TB), jnp.asarray(rsum))
-
-
-def sum_kernel(first_ref, got_ref, out_ref, total):
+        pair = first[2 * me + i] // 128
+        t = [recv[2 * pair + j // 2, j % 2] for j in range(4)]
+        return jnp.concatenate([jnp.concatenate(t[:2], 1), jnp.concatenate(t[2:], 1)], 0)
+
+    def put(i, d):
+        d = d.astype(bf16)
+        for core in range(2):
+            for q in range(4):
+                for slot in range(2):
+                    row = core * TS + q * 32
+                    grads[i, q, core, slot] = d[row : row + 32, slot * TS : slot * TS + TS]
+
+    compute(2, window, lambda i: target[i], spec, r, rt, sfreq, acc, field, inten, put, loss, level, rsum, 4, 4)
+    last = first[2 * me + 1] // 128
+
+    def stage(d, _):
+        which = jnp.where(last == d, 1, 0)
+        for q in range(4):
+            for core in range(2):
+                back[q * 32 + 2 * d + core] = grads[which, q, core]
+        return 0
+
+    lax.fori_loop(0, 16, stage, 0)
+
+    def send(k, _):
+        p, to = partner(k, plane, owner)
+        pltpu.make_async_remote_copy(src_ref=back.at[p * 32 + to], dst_ref=got.at[me], send_sem=bs, recv_sem=br,
+            device_id=(p, to), device_id_type=MESH).start()
+        return 0
+
+    lax.fori_loop(1, 128, send, 0)
+    own = pltpu.make_async_copy(back.at[me], got.at[me], ls)
+    own.start()
+    own.wait()
+    pltpu.make_async_copy(out.at[pl.ds(0, 31)], out.at[pl.ds(0, 31)], fs).wait()
+    pltpu.make_async_copy(back.at[pl.ds(0, 127)], back.at[pl.ds(0, 127)], bs).wait()
+    pltpu.make_async_copy(got.at[pl.ds(0, 127)], got.at[pl.ds(0, 127)], br).wait()
+
+
+def sum_kernel(first, got, out, total):
     chip = lax.axis_index("owner") // 2
     total[...] = jnp.zeros(total.shape, f32)
 
     def step(s, _):
-        for i in range(2):
-            first = first_ref[2 * s + i]
-
-            @pl.when(first // 128 == chip)
-            def _():
-                at = pl.multiple_of(first % 64 * 32, 32)
-                total[pl.ds(at, 32), :] += got_ref[s, 0].astype(f32)
-                total[pl.ds(at + 32, 32), :] += got_ref[s, 1].astype(f32)
-        return 0
-
-    lax.fori_loop(0, 128, step, 0)
+        near = first[2 * s]
+        far = first[2 * s + 1]
+        mine = jnp.where(near // 128 == chip, near, far)
+        column = jnp.where(mine // 128 == chip, jnp.minimum(lax.rem(mine, 64), 62), 64)
+        at = pl.ds(pl.multiple_of(column * 32, 32), 64)
+        total[at, :] += got[s].reshape(64, TS).astype(f32)
+        return 0
+
+    lax.fori_loop(0, 128, step, 0, unroll=4)
     for t in range(8):
         for j in range(32):
-            out_ref[8 * t : 8 * t + 8, 128 * j : 128 * j + 128] = total[pl.ds(256 * t + j, 8, stride=32), :]
+            out[8 * t : 8 * t + 8, 128 * j : 128 * j + 128] = total[pl.ds(256 * t + j, 8, stride=32), :]
 
 
 def body(mask_tiles, correlation, target, socs_kernels, socs_weights):
-    plane = lax.axis_index("clip")
-    owner = lax.axis_index("owner")
     first = correlation[:, 0]
-    near = lax.dynamic_slice(first, (plane * 64,), (64,)).reshape(32, 2)
-    hit = near // 128 == owner // 2
-    column = jnp.where(hit[:, 0], near[:, 0], near[:, 1]) % 64
-    column = jnp.minimum(column, 62)
-    outgoing = mask_tiles.reshape(64, TS, TS)[column[:, None] + jnp.arange(2)]
-    incoming = lax.all_to_all(outgoing, "owner", split_axis=0, concat_axis=0, tiled=True).reshape(64, TS, TS)
-    own = near[owner]
-    idx = (own[:, None] // 128 * 4 + jnp.arange(4)).reshape(8)
-    grads, losses = clip_grads(idx, socs_weights, incoming, target.reshape(2, W, W), socs_kernels.reshape(CH, KS, KS))
-    which = (jnp.arange(16) == own[1] // 128).astype(jnp.int32)
-    back = grads.reshape(2, 2, 2, 4, 32, TS)[which]
-    back = back.transpose(3, 0, 1, 2, 4, 5).reshape(128, 2, 32, TS)
-    got = lax.all_to_all(back, ("clip", "owner"), split_axis=0, concat_axis=0, tiled=True)
-    V=pl.BlockSpec(memory_space=pltpu.VMEM); S=pl.BlockSpec(memory_space=pltpu.SMEM)
+    Rb, RTb, T3, TB = tables()
+    rsum = np.broadcast_to(0.5 * Rb.astype(np.float32).sum(1, keepdims=True), (W, W)).copy()
+    V = pl.BlockSpec(memory_space=pltpu.VMEM)
+    S = pl.BlockSpec(memory_space=pltpu.SMEM)
+    A = pl.BlockSpec(memory_space=pl.ANY)
+    got, losses = pl.pallas_call(
+        step_kernel,
+        out_shape=(jax.ShapeDtypeStruct((128, 2, 32, TS), bf16), jax.ShapeDtypeStruct((2,), f32)),
+        in_specs=[S, S] + [V] * 8,
+        out_specs=(A, S),
+        scratch_shapes=[
+            pltpu.VMEM((32, 2, TS, TS), bf16),
+            pltpu.VMEM((32, 2, TS, TS), bf16),
+            pltpu.VMEM((128, 2, 32, TS), bf16),
+            pltpu.VMEM((2, 4, 2, 2, 32, TS), bf16),
+            pltpu.VMEM((CH, 16, 128), f32),
+            pltpu.VMEM((CH, 48, W), bf16),
+            pltpu.VMEM((CH, 4, HF, HF), f32),
+            pltpu.VMEM((2, 4, HF, HF), f32),
+            pltpu.VMEM((2, 4, HF, HF), f32),
+            pltpu.VMEM((CH, 2, W, W), f32),
+            pltpu.VMEM((2, W, W), f32),
+            pltpu.VMEM((CH, 1, W), f32),
+        ]
+        + [pltpu.SemaphoreType.DMA] * 5,
+        compiler_params=pltpu.CompilerParams(vmem_limit_bytes=56 * 2**20, collective_id=0, has_side_effects=True),
+    )(first, socs_weights, mask_tiles.reshape(64, TS, TS), target.reshape(2, W, W), socs_kernels.reshape(CH, KS, KS),
+        jnp.asarray(Rb), jnp.asarray(RTb), jnp.asarray(T3), jnp.asarray(TB), jnp.asarray(rsum))
     mask_grad = pl.pallas_call(sum_kernel, out_shape=jax.ShapeDtypeStruct((64, 4096), f32),
-        in_specs=[S, V], out_specs=V, scratch_shapes=[pltpu.VMEM((2048, 128), f32)],
+        in_specs=[S, V], out_specs=V, scratch_shapes=[pltpu.VMEM((66 * 32, TS), f32)],
     )(first, got)
     return mask_grad, losses
 

time: 110 us -> 109 us (level)
  Pallas kernels: 24.8 us -> 99.1 us
  blocking collectives: 37.4 us -> 0 us
  waiting for transfers between devices: 22.4 us -> 0 us
  starting transfers between devices: 9.73 us -> 0 us
  local copies, waits for them, and re-layouts: 11.9 us -> 8.53 us
  between operations: 3.37 us -> 0.65 us
    pallas_call x1, Pallas kernels: 16.9 us -> 93.9 us  [body(): pl.pallas_call(step_kernel, out_shape=(jax.ShapeDtypeStruct((128, 2, 32,...]
    all_to_all x1 -> x0, blocking collectives: 37.4 us -> none  [body(): lax.all_to_all(back, ('clip', 'owner'), split_axis=0, concat_axis=0, tile...]
    all_to_all x1 -> x0, waiting for transfers between devices: 22.4 us -> none  [body(): lax.all_to_all(outgoing, 'owner', split_axis=0, concat_axis=0, tiled=True)]
    all_to_all x1 -> x0, starting transfers between devices: 9.73 us -> none  [body(): lax.all_to_all(outgoing, 'owner', split_axis=0, concat_axis=0, tiled=True)]
    gather x2 -> x0, local copies, waits for them, and re-layouts: 4.05 us -> none  [the longest x1 2.15 us: body(): outgoing = mask_tiles.reshape(64, TS, TS)[column[:, None] + jnp.arange(2)]]
    pallas_call x1, Pallas kernels: 7.81 us -> 5.16 us  [body(): pl.pallas_call(sum_kernel, out_shape=jax.ShapeDtypeStruct((64, 4096), f32...]
    unnamed x11 -> x6, local copies, waits for them, and re-layouts: 4.93 us -> 7.27 us
  transfers between devices with their start and end apart: 1 -> 0, of which waited for: 1 -> 0; matrix products, arithmetic and copies ran while one was open for 3% -> 0% of each run, Pallas kernels for 0% -> 0%
where the time goes in v2:
time: 109 us; the launch traced here: 108 us
  Pallas kernels  99.1 us (91%)
  local copies, waits for them, and re-layouts  8.53 us (8%)
    pallas_call x1, Pallas kernels, body(): pl.pallas_call(step_kernel, out_shape=(jax.ShapeDtypeStruct((128, 2, 32,...  93.9 us
    unnamed x6, local copies, waits for them, and re-layouts  7.27 us
    pallas_call x1, Pallas kernels, body(): pl.pallas_call(sum_kernel, out_shape=jax.ShapeDtypeStruct((64, 4096), f32...  5.16 us

profile of v2, /device:TPU:1, one launch (start us, length us, event | category | flops | bytes accessed | tf_op | source)
XLA Modules:
  0.0 108.3 jit_solution(1994525500166117986)
XLA Ops:
  0.6 1.3 %slice.3 = s32[256,1]{0,1:T(1,128)} slice(s32[256,4]{0,1:T(4,128)} %param.11), slice={[0:256], [0:1]} | slice | bytes 2048 | tf_op jit(solution)/shard_map/slice | solution.py:207
  1.9 1.6 %copy.12 = f32[2,12,15,15]{3,2,1,0:T(8,128)} copy(f32[2,12,15,15]{3,0,2,1:T(2,128)} %param.13) | data formatting | bytes 43200 | tf_op args[3]
  3.5 1.7 %copy.16 = bf16[1,2,256,256]{3,2,1,0:T(8,128)(2,1)} copy(bf16[1,2,256,256]{3,1,2,0:T(2,128)(2,1)} %bitcast.12) | data formatting | bytes 524288
  5.2 3.5 %copy.13 = bf16[8,8,128,128]{3,2,1,0:T(8,128)(2,1)} copy(bf16[8,8,128,128]{3,1,2,0:T(8,128)(2,1)} %bitcast.9) | data formatting | bytes 4194304
  8.6 93.9 %shard_map.113 = (bf16[128,2,32,128]{3,2,1,0:T(8,128)(2,1)}, f32[2]{0:T(128)}) custom-call(s32[256]{0:T(256)} %bitcast.13, f32[12]{0:T(128)} %sw.1, bf16[64,128,128]{2,1,0:T(8,128)(2,1)} %bitcast.8, bf16[2,256,256]{2,1,0:T(8,128)(2,1)} %bitcast.10, f32[24,15,15]{2,1,0:T(8,128)} %bitcast.11, bf16[256,256]{1,0:T(8,128)(2,1)} %constant.10.clone.r, ...), custom_call_target="tpu_custom_call" | custom-call | tf_op jit(solution)/shard_map/pallas_call | solution.py:213
  102.6 0.0 copy-start
  102.6 5.2 %shard_map.114 = f32[64,4096]{1,0:T(8,128)} custom-call(s32[256]{0:T(256)} %bitcast.14, bf16[128,2,32,128]{3,2,1,0:T(8,128)(2,1)} %get-tuple-element.4.got), custom_call_target="tpu_custom_call" | custom-call | tf_op jit(solution)/shard_map/pallas_call | solution.py:236
  107.8 0.0 copy-done
  107.8 0.5 copy.18
Async XLA Ops:
  102.6 5.2 %copy-start = (f32[2]{0:T(128)S(1)}, f32[2]{0:T(128)}, u32[]{:S(2)}) copy-start(f32[2]{0:T(128)} %get-tuple-element.9) | copy-start | bytes 28

commit v3 on v2

v3 whole, which is shorter than its diff:
```python
import functools

import jax
import jax.numpy as jnp
import ml_dtypes
import numpy as np
from jax import lax
from jax.experimental import pallas as pl
from jax.experimental.pallas import tpu as pltpu
from jax.sharding import PartitionSpec as P

TS=128; W=256; HF=128; KS=15; AM=7; NK=12; CH=24
MESH = pl.DeviceIdType.MESH
f32=jnp.float32; bf16=jnp.bfloat16

def tables():
    u = np.arange(HF) + 0.5
    y = np.arange(W)
    ang = 2*np.pi*u[:,None]*y[None,:]/W
    R = np.concatenate([np.cos(ang), np.sin(ang)], 0)
    b = np.arange(KS)-AM
    ang2 = 2*np.pi*u[:,None]*b[None,:]/W
    T = np.concatenate([np.cos(ang2), np.sin(ang2)], 0)
    T16 = np.zeros((W,16)); T16[:,:KS]=T
    hi = T16.astype(np.float32).astype(ml_dtypes.bfloat16)
    lo = (T16-hi.astype(np.float64)).astype(np.float32).astype(ml_dtypes.bfloat16)
    T3 = np.concatenate([hi,hi,lo],1)
    TB = np.zeros((W, 128)); TB[:,:KS]=T
    TB = TB.T.astype(np.float32)
    Rb = R.astype(np.float32).astype(ml_dtypes.bfloat16)
    return Rb, np.ascontiguousarray(Rb.T), T3, TB

def dot(a,b):
    return jnp.dot(a,b,preferred_element_type=f32)


def quarters(s):
    return s[:HF, :HF], s[:HF, HF:], s[HF:, :HF], s[HF:, HF:]


def whole(cc, cs, sc, ss):
    return jnp.concatenate([jnp.concatenate([cc, cs], 1), jnp.concatenate([sc, ss], 1)], 0)


def step_kernel(unroll, first, sw, mask, target, taps, r, rt, t3, tb, rsum, got, loss,
        out, held0, held1, held2, held3, mid, recv0, recv1, grads, across, lines, back, pad, taph, spec, sfreq, acc, field, inten, level,
        s1s, s1r, s2s, s2r, xs, xr, gs, gr, bs, br, ls):
    held = (held0, held1, held2, held3)
    recv = (recv0, recv1)
    plane = lax.axis_index("clip")
    owner = lax.axis_index("owner")
    me = plane * 32 + owner
    chip = owner // 2
    core = owner % 2
    y = chip % 4
    z = chip // 4

    def at(route, a, b, c):
        return a * (8 - 6 * route) + b * (2 + 6 * route) + c

    def drain(ref, count, sem):
        part = ref.at[pl.ds(0, count)]
        pltpu.make_async_copy(part, part, sem).wait()

    def send(src, dst, send_sem, recv_sem, p, to):
        pltpu.make_async_remote_copy(src_ref=src, dst_ref=dst, send_sem=send_sem, recv_sem=recv_sem,
            device_id=(p, to), device_id_type=MESH).start()

    barrier = pltpu.get_barrier_semaphore()
    partners = [(plane, owner + 1 - 2 * core)]
    for j in (1, 2, 3):
        partners.append(((plane + j) % 4, owner))
        for c in range(2):
            partners.append((plane, at(0, (z + j) % 4, y, c)))
            partners.append((plane, at(0, z, (y + j) % 4, c)))
    for to in partners:
        pl.semaphore_signal(barrier, inc=1, device_id=to, device_id_type=MESH)

    a = z + core * (y - z)
    b = y + core * (z - y)

    def pick(k):
        b2 = (b + 1 + k) % 4

        def one(n, _):
            a2 = (a + n // 2) % 4
            c = n % 2
            dest = plane * 32 + at(core, a2, b2, c)
            near = first[2 * dest]
            far = first[2 * dest + 1]
            column = jnp.minimum(jnp.where(near >> 7 == chip, near, far) & 63, 62)
            slot = a2 * 8 + b2 * 2 + c
            out[slot, 0] = mask[column]
            out[slot, 1] = mask[column + 1]
            return 0

        lax.fori_loop(0, 8, one, 0)

    def first_stage(k):
        b2 = (b + 1 + k) % 4
        for j in (2, 1, 3):
            a2 = (a + j) % 4
            send(out.at[pl.ds(a2 * 8 + b2 * 2, 2)], held[k].at[pl.ds(a * 2, 2)], s1s, s1r.at[k],
                plane, at(core, a2, b, core))
        for c in range(2):
            held[k][a * 2 + c] = out[a * 8 + b2 * 2 + c]

    def second_stage(k):
        drain(held[k], 6, s1r.at[k])
        b2 = (b + 1 + k) % 4
        for i in range(2):
            for c in range(2):
                dest = plane * 32 + at(core, a, b2, c)
                pair = first[2 * dest + i] >> 7
                from_z = pair >> 2
                from_a = from_z + core * ((pair & 3) - from_z)
                mid[b2 * 4 + c * 2 + i] = held[k][from_a * 2 + c]
            if k < 3:
                for c in range(2):
                    send(mid.at[b2 * 4 + c * 2 + i], recv[i].at[core * 4 + b], s2s, s2r.at[i],
                        plane, at(core, a, b2, c))
            else:
                send(mid.at[b2 * 4 + (1 - core) * 2 + i], recv[i].at[core * 4 + b], s2s, s2r.at[i],
                    plane, owner + 1 - 2 * core)
                recv[i][core * 4 + b] = mid[b2 * 4 + core * 2 + i]

    pick(0)
    pl.semaphore_wait(barrier, len(partners))
    first_stage(0)
    for k in (1, 2, 3):
        pick(k)
        first_stage(k)

    pad[...] = jnp.zeros(pad.shape, f32)
    for c in range(CH):
        pad[c, :KS, :KS] = taps[c] * jnp.sqrt(sw[c % NK] * (1.0 / NK))
    level[...] = jnp.broadcast_to(
        jnp.sum(jnp.sum(pad[...], axis=1, keepdims=True), axis=2, keepdims=True) * 0.5, level.shape)
    m = jnp.dot(pad[...].reshape(CH * 16, 128), tb[...], precision=lax.Precision.HIGHEST,
        preferred_element_type=f32).reshape(CH, 16, W)
    high = m.astype(bf16)
    taph[:, 0:16, :] = high
    taph[:, 16:32, :] = (m - high.astype(f32)).astype(bf16)
    taph[:, 32:48, :] = high

    def spectrum(c, _):
        cc, cs, sc, ss = quarters(dot(t3[...], taph[c]))
        spec[c, 0] = cc - ss
        spec[c, 1] = sc + cs
        spec[c, 2] = cc + ss
        spec[c, 3] = sc - cs
        return 0

    for k in range(4):
        second_stage(k)
        if k < 3:
            lax.fori_loop(8 * k, 8 * k + 8, spectrum, 0, unroll=8)

    def transform(i):
        pair = first[2 * me + i] >> 7
        top = recv[i][pair & 3]
        low = recv[i][4 + (pair >> 2)]
        x = whole(top[0], top[1], low[0], low[1])
        t = (dot(r[...], x) - rsum[...]).astype(bf16)
        cc, cs, sc, ss = quarters(dot(t, rt[...]) * (0.5 / (HF * HF)))
        sfreq[0] = cc - ss
        sfreq[1] = sc + cs
        sfreq[2] = cc + ss
        sfreq[3] = sc - cs

    def back_to_pixels(aa, bb, a2, b2):
        u = dot(whole(aa + a2, bb - b2, bb + b2, a2 - aa).astype(bf16), r[...]).astype(bf16)
        return dot(rt[...], u)

    def forward():
        inten[...] = jnp.zeros((W, W), f32)

        def channel(c, _):
            p, q, p2, q2 = (sfreq[j] for j in range(4))
            m, n, m2, n2 = (spec[c, j] for j in range(4))
            e = back_to_pixels(p * m - q * n, p * n + q * m, p2 * m2 - q2 * n2, p2 * n2 + q2 * m2) + level[c]
            field[c] = e
            inten[...] = inten[...] + e * e
            return 0

        lax.fori_loop(0, CH, channel, 0, unroll=unroll)

    def resist(i):
        row = lax.broadcasted_iota(jnp.int32, (W, W), 0)
        col = lax.broadcasted_iota(jnp.int32, (W, W), 1)
        inside = (row >= AM) & (row < W - AM) & (col >= AM) & (col < W - AM)
        level_at = 1.0 / (1.0 + jnp.exp(-10.0 * (inten[...] - 0.3)))
        miss = jnp.where(inside, level_at - target[i].astype(f32), 0.0)
        loss[i] = jnp.sum(miss * miss) * (1.0 / ((W - 2 * AM) ** 2))
        inten[...] = 40.0 * miss * level_at * (1.0 - level_at)

    def backward():
        acc[...] = jnp.zeros(acc.shape, f32)

        def channel(c, _):
            g = (inten[...] * field[c]).astype(bf16)
            v = dot(g, rt[...]).astype(bf16)
            cc, cs, sc, ss = quarters(dot(r[...], v))
            p, q, p2, q2 = cc - ss, sc + cs, cc + ss, sc - cs
            m, n, m2, n2 = (spec[c, j] for j in range(4))
            acc[0] += p * m + q * n
            acc[1] += q * m - p * n
            acc[2] += p2 * m2 + q2 * n2
            acc[3] += q2 * m2 - p2 * n2
            return 0

        lax.fori_loop(0, CH, channel, 0, unroll=unroll)

    def finish(i):
        d = back_to_pixels(*(acc[j] * (0.5 / (HF * HF)) for j in range(4))).astype(bf16)
        for q in range(4):
            for part in range(2):
                for slot in range(2):
                    row = part * TS + q * 32
                    grads[i * 8 + q * 2 + part, slot] = d[row : row + 32, slot * TS : slot * TS + TS]

    def to_planes(i):
        for j in (1, 2, 3):
            p = (plane + j) % 4
            for part in range(2):
                send(grads.at[i * 8 + p * 2 + part], across.at[i * 8 + part * 4 + plane], xs, xr.at[i], p, owner)
        for part in range(2):
            across[i * 8 + part * 4 + plane] = grads[i * 8 + plane * 2 + part]

    def to_line(i):
        drain(across, 6, xr.at[i])
        for j in (2, 1, 3):
            for part in range(2):
                pa, pb = (z, y) if part == 0 else (y, z)
                here = across.at[pl.ds(i * 8 + part * 4, 4)]
                send(here, lines.at[pl.ds(part * 32 + pa * 8 + i * 4, 4)], gs, gr.at[i],
                    plane, at(part, (pa + j) % 4, pb, core))
        for part in range(2):
            pa = z if part == 0 else y
            lines[pl.ds(part * 32 + pa * 8 + i * 4, 4)] = across[pl.ds(i * 8 + part * 4, 4)]

    def to_owners(j, part):
        pa, pb = (z, y) if part == 0 else (y, z)
        b2 = (pb + j) % 4
        goal = pa * 4 + b2 if part == 0 else b2 * 4 + pa

        def one(n, _):
            a_src = n // 4
            x_src = n % 4
            source = x_src * 32 + at(part, a_src, pb, core)
            which = jnp.where(first[2 * source + 1] >> 7 == goal, 1, 0)
            back[part * 64 + b2 * 16 + n] = lines[part * 32 + a_src * 8 + which * 4 + x_src]
            return 0

        lax.fori_loop(0, 16, one, 0, unroll=2)
        src = back.at[pl.ds(part * 64 + b2 * 16, 16)]
        dst = got.at[pl.ds((pb * 2 + core) * 16, 16)]
        if j:
            send(src, dst, bs, br, plane, at(part, pa, b2, part))
        else:

            @pl.when(core == part)
            def _():
                pltpu.make_async_copy(src, dst, ls).start()

            @pl.when(core != part)
            def _():
                send(src, dst, bs, br, plane, owner + 1 - 2 * core)

    drain(recv[0], 7, s2r.at[0])
    transform(0)
    forward()
    resist(0)
    backward()
    finish(0)
    to_planes(0)
    drain(recv[1], 7, s2r.at[1])
    transform(1)
    forward()
    to_line(0)
    resist(1)
    backward()
    finish(1)
    to_planes(1)
    to_line(1)
    drain(lines, 24, gr.at[0])
    drain(lines, 24, gr.at[1])
    for j in (2, 1, 3, 0):
        for part in range(2):
            to_owners(j, part)
    drain(out, 24, s1s)
    drain(mid, 14, s2s)
    drain(grads, 12, xs)
    drain(lines, 48, gs)
    drain(back, 112, bs)
    drain(got, 16, ls)
    drain(got, 112, br)


def sum_kernel(first, losses, got, out, loss, total):
    owner = lax.axis_index("owner")
    chip = owner // 2
    core = owner % 2
    total[...] = jnp.zeros(total.shape, f32)

    def step(s, _):
        source = (s & 3) * 32 + ((s >> 2) & 3) * (8 - 6 * core) + (s >> 5) * (2 + 6 * core) + ((s >> 4) & 1)
        near = first[2 * source]
        far = first[2 * source + 1]
        mine = jnp.where(near >> 7 == chip, near, far)
        column = jnp.where(mine >> 7 == chip, jnp.minimum(mine & 63, 62), 64)
        at = pl.ds(pl.multiple_of(column * 32, 32), 64)
        total[at, :] += got[s].reshape(64, TS).astype(f32)
        return 0

    lax.fori_loop(0, 128, step, 0, unroll=4)
    for t in range(8):
        for j in range(32):
            out[8 * t : 8 * t + 8, 128 * j : 128 * j + 128] = total[pl.ds(256 * t + j, 8, stride=32), :]
    for i in range(2):
        loss[i] = losses[i]


def body(mask_tiles, correlation, target, socs_kernels, socs_weights):
    first = correlation[:, 0]
    Rb, RTb, T3, TB = tables()
    rsum = np.broadcast_to(0.5 * Rb.astype(np.float32).sum(1, keepdims=True), (W, W)).copy()
    V = pl.BlockSpec(memory_space=pltpu.VMEM)
    S = pl.BlockSpec(memory_space=pltpu.SMEM)
    A = pl.BlockSpec(memory_space=pl.ANY)
    D = pltpu.SemaphoreType.DMA
    got, losses = pl.pallas_call(
        functools.partial(step_kernel, 8),
        out_shape=(jax.ShapeDtypeStruct((128, 2, 32, TS), bf16), jax.ShapeDtypeStruct((2,), f32)),
        in_specs=[S, S] + [V] * 8,
        out_specs=(A, S),
        scratch_shapes=[
            pltpu.VMEM((32, 2, TS, TS), bf16),
            *[pltpu.VMEM((8, 2, TS, TS), bf16)] * 4,
            pltpu.VMEM((16, 2, TS, TS), bf16),
            *[pltpu.VMEM((8, 2, TS, TS), bf16)] * 2,
            pltpu.VMEM((16, 2, 32, TS), bf16),
            pltpu.VMEM((16, 2, 32, TS), bf16),
            pltpu.VMEM((64, 2, 32, TS), bf16),
            pltpu.VMEM((128, 2, 32, TS), bf16),
            pltpu.VMEM((CH, 16, 128), f32),
            pltpu.VMEM((CH, 48, W), bf16),
            pltpu.VMEM((CH, 4, HF, HF), f32),
            pltpu.VMEM((4, HF, HF), f32),
            pltpu.VMEM((4, HF, HF), f32),
            pltpu.VMEM((CH, W, W), f32),
            pltpu.VMEM((W, W), f32),
            pltpu.VMEM((CH, 1, W), f32),
            D, D((4,)), D, D((2,)), D, D((2,)), D, D((2,)), D, D, D,
        ],
        compiler_params=pltpu.CompilerParams(vmem_limit_bytes=56 * 2**20, collective_id=0, has_side_effects=True),
    )(first, socs_weights, mask_tiles.reshape(64, TS, TS), target.reshape(2, W, W), socs_kernels.reshape(CH, KS, KS),
        jnp.asarray(Rb), jnp.asarray(RTb), jnp.asarray(T3), jnp.asarray(TB), jnp.asarray(rsum))
    return pl.pallas_call(sum_kernel,
        out_shape=(jax.ShapeDtypeStruct((64, 4096), f32), jax.ShapeDtypeStruct((2,), f32)),
        in_specs=[S, S, V], out_specs=(V, S), scratch_shapes=[pltpu.VMEM((66 * 32, TS), f32)],
    )(first, losses, got)


def solution(mesh):
    placed = (P("owner", None), P(), P(("clip", "owner"), None), P(), P())
    return jax.shard_map(body, mesh=mesh, in_specs=placed,
        out_specs=(P("owner", "clip"), P(("clip", "owner"))), check_vma=False)
```

time: 109 us -> 80.9 us (0.74)
  Pallas kernels: 99.1 us -> 71.9 us
    pallas_call x2, Pallas kernels: 99.1 us -> 71.9 us  [the longest x1 67.4 us: body(): pl.pallas_call(functools.partial(step_kernel, 8), out_shape=(jax.ShapeDty...]
    unnamed x6 -> x3, local copies, waits for them, and re-layouts: 7.27 us -> 6.77 us
where the time goes in v3:
time: 80.9 us; the launch traced here: 80.6 us
  Pallas kernels  71.9 us (89%)
  local copies, waits for them, and re-layouts  8.05 us (10%)
    pallas_call x1, Pallas kernels, body(): pl.pallas_call(functools.partial(step_kernel, 8), out_shape=(jax.ShapeDty...  67.4 us
    unnamed x3, local copies, waits for them, and re-layouts  6.77 us
    pallas_call x1, Pallas kernels, body(): pl.pallas_call(sum_kernel, out_shape=(jax.ShapeDtypeStruct((64, 4096), f3...  4.51 us

profile of v3, /device:TPU:1, one launch (start us, length us, event | category | flops | bytes accessed | tf_op | source)
XLA Modules:
  0.0 80.6 jit_solution(12118410300372675201)
XLA Ops:
  0.6 1.3 %slice.3 = s32[256,1]{0,1:T(1,128)} slice(s32[256,4]{0,1:T(4,128)} %param.11), slice={[0:256], [0:1]} | slice | bytes 2048 | tf_op jit(solution)/shard_map/slice | solution.py:325
  1.9 1.6 %copy.12 = f32[2,12,15,15]{3,2,1,0:T(8,128)} copy(f32[2,12,15,15]{3,0,2,1:T(2,128)} %param.13) | data formatting | bytes 43200 | tf_op args[3]
  3.5 1.7 %copy.16 = bf16[1,2,256,256]{3,2,1,0:T(8,128)(2,1)} copy(bf16[1,2,256,256]{3,1,2,0:T(2,128)(2,1)} %bitcast.12) | data formatting | bytes 524288
  5.2 3.5 %copy.13 = bf16[8,8,128,128]{3,2,1,0:T(8,128)(2,1)} copy(bf16[8,8,128,128]{3,1,2,0:T(8,128)(2,1)} %bitcast.9) | data formatting | bytes 4194304
  8.7 67.4 %shard_map.113 = (bf16[128,2,32,128]{3,2,1,0:T(8,128)(2,1)}, f32[2]{0:T(128)}) custom-call(s32[256]{0:T(256)} %bitcast.13, f32[12]{0:T(128)} %sw.1, bf16[64,128,128]{2,1,0:T(8,128)(2,1)} %bitcast.8, bf16[2,256,256]{2,1,0:T(8,128)(2,1)} %bitcast.10, f32[24,15,15]{2,1,0:T(8,128)} %bitcast.11, bf16[256,256]{1,0:T(8,128)(2,1)} %constant.10.clone.r, ...), custom_call_target="tpu_custom_call" | custom-call | tf_op jit(solution)/shard_map/pallas_call | solution.py:332
  76.1 4.5 %shard_map.114 = (f32[64,4096]{1,0:T(8,128)}, f32[2]{0:T(128)}) custom-call(s32[256]{0:T(256)} %bitcast.14, f32[2]{0:T(128)} %get-tuple-element.4.losses, bf16[128,2,32,128]{3,2,1,0:T(8,128)(2,1)} %get-tuple-element.5.got), custom_call_target="tpu_custom_call" | custom-call | tf_op jit(solution)/shard_map/pallas_call | solution.py:359

commit v4 on v3

--- a/solution.py
+++ b/solution.py
@@ -42,9 +42,9 @@
     return jnp.concatenate([jnp.concatenate([cc, cs], 1), jnp.concatenate([sc, ss], 1)], 0)
 
 
-def step_kernel(unroll, first, sw, mask, target, taps, r, rt, t3, tb, rsum, got, loss,
-        out, held0, held1, held2, held3, mid, recv0, recv1, grads, across, lines, back, pad, taph, spec, sfreq, acc, field, inten, level,
-        s1s, s1r, s2s, s2r, xs, xr, gs, gr, bs, br, ls):
+def step_kernel(unroll, first, sw, mask_in, target_in, taps_in, r_in, rt_in, t3_in, tb_in, got, loss,
+        raw, mask, wide, target, taps, r, rt, t3, tb, rsum, out, held0, held1, held2, held3, mid, recv0, recv1, grads, across, lines, back, pad, taph, spec, sfreq, acc, field, inten, level,
+        ins, s1s, s1r, s2s, s2r, xs, xr, gs, gr, bs, br, ls):
     held = (held0, held1, held2, held3)
     recv = (recv0, recv1)
     plane = lax.axis_index("clip")
@@ -76,6 +76,14 @@
     for to in partners:
         pl.semaphore_signal(barrier, inc=1, device_id=to, device_id_type=MESH)
 
+    loads = [pltpu.make_async_copy(mask_in.at[pl.ds(16 * n, 16)], raw.at[pl.ds(16 * n, 16)], ins.at[n]) for n in range(4)]
+    loads += [
+        pltpu.make_async_copy(src, dst, ins.at[4 + n])
+        for n, (src, dst) in enumerate(((taps_in, taps), (tb_in, tb), (t3_in, t3), (target_in, wide), (r_in, r), (rt_in, rt)))
+    ]
+    for load in loads:
+        load.start()
+
     a = z + core * (y - z)
     b = y + core * (z - y)
 
@@ -86,12 +94,12 @@
             a2 = (a + n // 2) % 4
             c = n % 2
             dest = plane * 32 + at(core, a2, b2, c)
-            near = first[2 * dest]
-            far = first[2 * dest + 1]
+            near = first[0, 2 * dest]
+            far = first[0, 2 * dest + 1]
             column = jnp.minimum(jnp.where(near >> 7 == chip, near, far) & 63, 62)
             slot = a2 * 8 + b2 * 2 + c
-            out[slot, 0] = mask[column]
-            out[slot, 1] = mask[column + 1]
+            for n2 in range(2):
+                out[slot, n2] = mask[column + n2].astype(bf16)
             return 0
 
         lax.fori_loop(0, 8, one, 0)
@@ -105,13 +113,14 @@
         for c in range(2):
             held[k][a * 2 + c] = out[a * 8 + b2 * 2 + c]
 
-    def second_stage(k):
-        drain(held[k], 6, s1r.at[k])
+    def second_stage(k, i):
+        if i == 0:
+            drain(held[k], 6, s1r.at[k])
         b2 = (b + 1 + k) % 4
-        for i in range(2):
+        if True:
             for c in range(2):
                 dest = plane * 32 + at(core, a, b2, c)
-                pair = first[2 * dest + i] >> 7
+                pair = first[0, 2 * dest + i] >> 7
                 from_z = pair >> 2
                 from_a = from_z + core * ((pair & 3) - from_z)
                 mid[b2 * 4 + c * 2 + i] = held[k][from_a * 2 + c]
@@ -124,6 +133,18 @@
                     plane, owner + 1 - 2 * core)
                 recv[i][core * 4 + b] = mid[b2 * 4 + core * 2 + i]
 
+    flat = mask.reshape(64 * TS, TS)
+    for n in range(4):
+        loads[n].wait()
+
+        def rows(j, _):
+            v = raw[16 * n : 16 * n + 16, pl.ds(pl.multiple_of(j * TS, TS), TS)].astype(f32)
+            flat[pl.ds(16 * n * TS + j, 8, stride=TS), :] = v[:8]
+            flat[pl.ds((16 * n + 8) * TS + j, 8, stride=TS), :] = v[8:]
+            return 0
+
+        lax.fori_loop(0, TS, rows, 0, unroll=8)
+
     pick(0)
     pl.semaphore_wait(barrier, len(partners))
     first_stage(0)
@@ -131,9 +152,11 @@
         pick(k)
         first_stage(k)
 
+    for load in loads[4:7]:
+        load.wait()
     pad[...] = jnp.zeros(pad.shape, f32)
     for c in range(CH):
-        pad[c, :KS, :KS] = taps[c] * jnp.sqrt(sw[c % NK] * (1.0 / NK))
+        pad[c, :KS, :KS] = taps[c % NK, :, c // NK, :] * jnp.sqrt(sw[c % NK] * (1.0 / NK))
     level[...] = jnp.broadcast_to(
         jnp.sum(jnp.sum(pad[...], axis=1, keepdims=True), axis=2, keepdims=True) * 0.5, level.shape)
     m = jnp.dot(pad[...].reshape(CH * 16, 128), tb[...], precision=lax.Precision.HIGHEST,
@@ -152,12 +175,24 @@
         return 0
 
     for k in range(4):
-        second_stage(k)
+        second_stage(k, 0)
         if k < 3:
             lax.fori_loop(8 * k, 8 * k + 8, spectrum, 0, unroll=8)
 
+    for k in range(4):
+        second_stage(k, 1)
+    for load in loads[7:]:
+        load.wait()
+
+    def widen(n, _):
+        target[pl.ds(n, 2, stride=2 * W), :] = wide[:, pl.ds(pl.multiple_of(n * TS, TS), TS)].astype(f32)
+        return 0
+
+    lax.fori_loop(0, 2 * W, widen, 0, unroll=8)
+    rsum[...] = dot(r[...], jnp.full((W, W), 0.5, bf16))
+
     def transform(i):
-        pair = first[2 * me + i] >> 7
+        pair = first[0, 2 * me + i] >> 7
         top = recv[i][pair & 3]
         low = recv[i][4 + (pair >> 2)]
         x = whole(top[0], top[1], low[0], low[1])
@@ -190,7 +225,8 @@
         col = lax.broadcasted_iota(jnp.int32, (W, W), 1)
         inside = (row >= AM) & (row < W - AM) & (col >= AM) & (col < W - AM)
         level_at = 1.0 / (1.0 + jnp.exp(-10.0 * (inten[...] - 0.3)))
-        miss = jnp.where(inside, level_at - target[i].astype(f32), 0.0)
+        goal = jnp.concatenate([target[pl.ds(i * 2 * W + n, W, stride=2), :] for n in range(2)], 1)
+        miss = jnp.where(inside, level_at - goal, 0.0)
         loss[i] = jnp.sum(miss * miss) * (1.0 / ((W - 2 * AM) ** 2))
         inten[...] = 40.0 * miss * level_at * (1.0 - level_at)
 
@@ -248,7 +284,7 @@
             a_src = n // 4
             x_src = n % 4
             source = x_src * 32 + at(part, a_src, pb, core)
-            which = jnp.where(first[2 * source + 1] >> 7 == goal, 1, 0)
+            which = jnp.where(first[0, 2 * source + 1] >> 7 == goal, 1, 0)
             back[part * 64 + b2 * 16 + n] = lines[part * 32 + a_src * 8 + which * 4 + x_src]
             return 0
 
@@ -305,8 +341,8 @@
 
     def step(s, _):
         source = (s & 3) * 32 + ((s >> 2) & 3) * (8 - 6 * core) + (s >> 5) * (2 + 6 * core) + ((s >> 4) & 1)
-        near = first[2 * source]
-        far = first[2 * source + 1]
+        near = first[0, 2 * source]
+        far = first[0, 2 * source + 1]
         mine = jnp.where(near >> 7 == chip, near, far)
         column = jnp.where(mine >> 7 == chip, jnp.minimum(mine & 63, 62), 64)
         at = pl.ds(pl.multiple_of(column * 32, 32), 64)
@@ -322,9 +358,8 @@
 
 
 def body(mask_tiles, correlation, target, socs_kernels, socs_weights):
-    first = correlation[:, 0]
+    first = correlation.T
     Rb, RTb, T3, TB = tables()
-    rsum = np.broadcast_to(0.5 * Rb.astype(np.float32).sum(1, keepdims=True), (W, W)).copy()
     V = pl.BlockSpec(memory_space=pltpu.VMEM)
     S = pl.BlockSpec(memory_space=pltpu.SMEM)
     A = pl.BlockSpec(memory_space=pl.ANY)
@@ -332,9 +367,19 @@
     got, losses = pl.pallas_call(
         functools.partial(step_kernel, 8),
         out_shape=(jax.ShapeDtypeStruct((128, 2, 32, TS), bf16), jax.ShapeDtypeStruct((2,), f32)),
-        in_specs=[S, S] + [V] * 8,
+        in_specs=[S, S] + [A] * 7,
         out_specs=(A, S),
         scratch_shapes=[
+            pltpu.VMEM((64, TS * TS), bf16),
+            pltpu.VMEM((64, TS, TS), f32),
+            pltpu.VMEM((2, W * W), bf16),
+            pltpu.VMEM((4 * W, TS), f32),
+            pltpu.VMEM((NK, KS, 2, KS), f32),
+            pltpu.VMEM((W, W), bf16),
+            pltpu.VMEM((W, W), bf16),
+            pltpu.VMEM((W, 48), bf16),
+            pltpu.VMEM((128, W), f32),
+            pltpu.VMEM((W, W), f32),
             pltpu.VMEM((32, 2, TS, TS), bf16),
             *[pltpu.VMEM((8, 2, TS, TS), bf16)] * 4,
             pltpu.VMEM((16, 2, TS, TS), bf16),
@@ -351,11 +396,11 @@
             pltpu.VMEM((CH, W, W), f32),
             pltpu.VMEM((W, W), f32),
             pltpu.VMEM((CH, 1, W), f32),
-            D, D((4,)), D, D((2,)), D, D((2,)), D, D((2,)), D, D, D,
+            D((10,)), D, D((4,)), D, D((2,)), D, D((2,)), D, D((2,)), D, D, D,
         ],
         compiler_params=pltpu.CompilerParams(vmem_limit_bytes=56 * 2**20, collective_id=0, has_side_effects=True),
-    )(first, socs_weights, mask_tiles.reshape(64, TS, TS), target.reshape(2, W, W), socs_kernels.reshape(CH, KS, KS),
-        jnp.asarray(Rb), jnp.asarray(RTb), jnp.asarray(T3), jnp.asarray(TB), jnp.asarray(rsum))
+    )(first, socs_weights, mask_tiles, target, socs_kernels.transpose(1, 2, 0, 3),
+        jnp.asarray(Rb), jnp.asarray(RTb), jnp.asarray(T3), jnp.asarray(TB))
     return pl.pallas_call(sum_kernel,
         out_shape=(jax.ShapeDtypeStruct((64, 4096), f32), jax.ShapeDtypeStruct((2,), f32)),
         in_specs=[S, S, V], out_specs=(V, S), scratch_shapes=[pltpu.VMEM((66 * 32, TS), f32)],

time: 80.9 us -> 73.9 us (0.913)
  local copies, waits for them, and re-layouts: 8.05 us -> 0 us
  Pallas kernels: 71.9 us -> 73.1 us
    unnamed x3 -> x0, local copies, waits for them, and re-layouts: 6.77 us -> none
    slice x1 -> x0, local copies, waits for them, and re-layouts: 1.28 us -> none  [body(): first = correlation[:, 0]]
    pallas_call x1, Pallas kernels: 67.4 us -> 68.3 us  [body(): pl.pallas_call(functools.partial(step_kernel, 8), out_shape=(jax.ShapeDty...]
where the time goes in v4:
time: 73.9 us; the launch traced here: 73.7 us
  Pallas kernels  73.1 us (99%)
    pallas_call x1, Pallas kernels, body(): pl.pallas_call(functools.partial(step_kernel, 8), out_shape=(jax.ShapeDty...  68.3 us
    pallas_call x1, Pallas kernels, body(): pl.pallas_call(sum_kernel, out_shape=(jax.ShapeDtypeStruct((64, 4096), f3...  4.8 us

profile of v4, /device:TPU:1, one launch (start us, length us, event | category | flops | bytes accessed | tf_op | source)
XLA Modules:
  0.0 73.7 jit_solution(8494952741225156755)
XLA Ops:
  0.6 68.3 %shard_map.104 = (bf16[128,2,32,128]{3,2,1,0:T(8,128)(2,1)}, f32[2]{0:T(128)}) custom-call(s32[4,256]{1,0:T(4,128)} %bitcast.3, f32[12]{0:T(128)} %sw.1, bf16[64,16384]{1,0:T(8,128)(2,1)} %mask_in.1, bf16[2,65536]{1,0:T(2,128)(2,1)} %target_in.1, f32[12,15,2,15]{3,2,1,0:T(2,128)} %bitcast.2, bf16[256,256]{1,0:T(8,128)(2,1)} %constant.8.clone.r_in, ...), custom_call_target="tpu_custom_call" | custom-call | tf_op jit(solution)/shard_map/pallas_call | solution.py:367
  68.9 4.8 %shard_map.105 = (f32[64,4096]{1,0:T(8,128)}, f32[2]{0:T(128)}) custom-call(s32[4,256]{1,0:T(4,128)} %bitcast.4, f32[2]{0:T(128)} %get-tuple-element.4.losses, bf16[128,2,32,128]{3,2,1,0:T(8,128)(2,1)} %get-tuple-element.5.got), custom_call_target="tpu_custom_call" | custom-call | tf_op jit(solution)/shard_map/pallas_call | solution.py:404

commit v5 on v4

--- a/solution.py
+++ b/solution.py
@@ -10,6 +10,7 @@
 from jax.sharding import PartitionSpec as P
 
 TS=128; W=256; HF=128; KS=15; AM=7; NK=12; CH=24
+PITCH = 136
 MESH = pl.DeviceIdType.MESH
 f32=jnp.float32; bf16=jnp.bfloat16
 
@@ -43,7 +44,7 @@
 
 
 def step_kernel(unroll, first, sw, mask_in, target_in, taps_in, r_in, rt_in, t3_in, tb_in, got, loss,
-        raw, mask, wide, target, taps, r, rt, t3, tb, rsum, out, held0, held1, held2, held3, mid, recv0, recv1, grads, across, lines, back, pad, taph, spec, sfreq, acc, field, inten, level,
+        raw, mask, wide, target, taps, r, rt, t3, tb, rsum, out, held0, held1, held2, held3, mid, recv0, recv1, grads, across, lines, back, pad, taph, spec, sfreq, acc, field, inten, level, flow, amp,
         ins, s1s, s1r, s2s, s2r, xs, xr, gs, gr, bs, br, ls):
     held = (held0, held1, held2, held3)
     recv = (recv0, recv1)
@@ -99,7 +100,7 @@
             column = jnp.minimum(jnp.where(near >> 7 == chip, near, far) & 63, 62)
             slot = a2 * 8 + b2 * 2 + c
             for n2 in range(2):
-                out[slot, n2] = mask[column + n2].astype(bf16)
+                out[slot, n2] = mask[column + n2, :TS].astype(bf16)
             return 0
 
         lax.fori_loop(0, 8, one, 0)
@@ -133,14 +134,14 @@
                     plane, owner + 1 - 2 * core)
                 recv[i][core * 4 + b] = mid[b2 * 4 + core * 2 + i]
 
-    flat = mask.reshape(64 * TS, TS)
+    flat = mask.reshape(64 * PITCH, TS)
     for n in range(4):
         loads[n].wait()
 
         def rows(j, _):
             v = raw[16 * n : 16 * n + 16, pl.ds(pl.multiple_of(j * TS, TS), TS)].astype(f32)
-            flat[pl.ds(16 * n * TS + j, 8, stride=TS), :] = v[:8]
-            flat[pl.ds((16 * n + 8) * TS + j, 8, stride=TS), :] = v[8:]
+            flat[pl.ds(16 * n * PITCH + j, 8, stride=PITCH), :] = v[:8]
+            flat[pl.ds((16 * n + 8) * PITCH + j, 8, stride=PITCH), :] = v[8:]
             return 0
 
         lax.fori_loop(0, TS, rows, 0, unroll=8)
@@ -156,10 +157,11 @@
         load.wait()
     pad[...] = jnp.zeros(pad.shape, f32)
     for c in range(CH):
-        pad[c, :KS, :KS] = taps[c % NK, :, c // NK, :] * jnp.sqrt(sw[c % NK] * (1.0 / NK))
-    level[...] = jnp.broadcast_to(
-        jnp.sum(jnp.sum(pad[...], axis=1, keepdims=True), axis=2, keepdims=True) * 0.5, level.shape)
-    m = jnp.dot(pad[...].reshape(CH * 16, 128), tb[...], precision=lax.Precision.HIGHEST,
+        pad[c, :KS, :KS] = taps[c % NK, :, c // NK, :]
+        amp[c] = jnp.full((1, W), jnp.sqrt(sw[c % NK] * (1.0 / NK)))
+    flow[...] = jnp.broadcast_to(
+        jnp.sum(jnp.sum(pad[...], axis=1, keepdims=True), axis=2, keepdims=True), flow.shape)
+    m = jnp.dot((pad[...] * amp[:, :, :128]).reshape(CH * 16, 128), tb[...], precision=lax.Precision.HIGHEST,
         preferred_element_type=f32).reshape(CH, 16, W)
     high = m.astype(bf16)
     taph[:, 0:16, :] = high
@@ -189,14 +191,18 @@
         return 0
 
     lax.fori_loop(0, 2 * W, widen, 0, unroll=8)
-    rsum[...] = dot(r[...], jnp.full((W, W), 0.5, bf16))
+    rsum[...] = dot(r[...], jnp.full((W, W), 1.0, bf16))
 
     def transform(i):
         pair = first[0, 2 * me + i] >> 7
         top = recv[i][pair & 3]
         low = recv[i][4 + (pair >> 2)]
         x = whole(top[0], top[1], low[0], low[1])
-        t = (dot(r[...], x) - rsum[...]).astype(bf16)
+        sums = jnp.sum(x.astype(f32), axis=0, keepdims=True)
+        rounded = sums.astype(bf16).astype(f32)
+        t = (dot(r[...], x) - rsum[...] * (0.5 - (rounded - sums) * (1.0 / W))).astype(bf16)
+        zero = flow[...] * jnp.sum(rounded)
+        level[...] = amp[...] * (0.5 * flow[...] + (zero.astype(bf16).astype(f32) - zero) * (1.0 / (W * W)))
         cc, cs, sc, ss = quarters(dot(t, rt[...]) * (0.5 / (HF * HF)))
         sfreq[0] = cc - ss
         sfreq[1] = sc + cs
@@ -333,10 +339,13 @@
     drain(got, 112, br)
 
 
-def sum_kernel(first, losses, got, out, loss, total):
+def sum_kernel(first, losses, got, out, loss, held, total, rows, ins, outs):
     owner = lax.axis_index("owner")
     chip = owner // 2
     core = owner % 2
+    loads = [pltpu.make_async_copy(got.at[pl.ds(16 * n, 16)], held.at[pl.ds(16 * n, 16)], ins.at[n]) for n in range(8)]
+    for load in loads:
+        load.start()
     total[...] = jnp.zeros(total.shape, f32)
 
     def step(s, _):
@@ -345,22 +354,29 @@
         far = first[0, 2 * source + 1]
         mine = jnp.where(near >> 7 == chip, near, far)
         column = jnp.where(mine >> 7 == chip, jnp.minimum(mine & 63, 62), 64)
-        at = pl.ds(pl.multiple_of(column * 32, 32), 64)
-        total[at, :] += got[s].reshape(64, TS).astype(f32)
+        for n in range(2):
+            total[pl.ds(pl.multiple_of((column + n) * 40, 8), 32), :] += held[s, n].astype(f32)
         return 0
 
-    lax.fori_loop(0, 128, step, 0, unroll=4)
+    for n in range(8):
+        loads[n].wait()
+        lax.fori_loop(16 * n, 16 * n + 16, step, 0, unroll=4)
+    stores = []
     for t in range(8):
         for j in range(32):
-            out[8 * t : 8 * t + 8, 128 * j : 128 * j + 128] = total[pl.ds(256 * t + j, 8, stride=32), :]
+            rows[8 * t : 8 * t + 8, 128 * j : 128 * j + 128] = total[pl.ds(320 * t + j, 8, stride=40), :]
+        store = pltpu.make_async_copy(rows.at[pl.ds(8 * t, 8)], out.at[pl.ds(8 * t, 8)], outs.at[t])
+        store.start()
+        stores.append(store)
     for i in range(2):
         loss[i] = losses[i]
+    for store in stores:
+        store.wait()
 
 
 def body(mask_tiles, correlation, target, socs_kernels, socs_weights):
     first = correlation.T
     Rb, RTb, T3, TB = tables()
-    V = pl.BlockSpec(memory_space=pltpu.VMEM)
     S = pl.BlockSpec(memory_space=pltpu.SMEM)
     A = pl.BlockSpec(memory_space=pl.ANY)
     D = pltpu.SemaphoreType.DMA
@@ -371,7 +387,7 @@
         out_specs=(A, S),
         scratch_shapes=[
             pltpu.VMEM((64, TS * TS), bf16),
-            pltpu.VMEM((64, TS, TS), f32),
+            pltpu.VMEM((64, PITCH, TS), f32),
             pltpu.VMEM((2, W * W), bf16),
             pltpu.VMEM((4 * W, TS), f32),
             pltpu.VMEM((NK, KS, 2, KS), f32),
@@ -395,7 +411,7 @@
             pltpu.VMEM((4, HF, HF), f32),
             pltpu.VMEM((CH, W, W), f32),
             pltpu.VMEM((W, W), f32),
-            pltpu.VMEM((CH, 1, W), f32),
+            *[pltpu.VMEM((CH, 1, W), f32)] * 3,
             D((10,)), D, D((4,)), D, D((2,)), D, D((2,)), D, D((2,)), D, D, D,
         ],
         compiler_params=pltpu.CompilerParams(vmem_limit_bytes=56 * 2**20, collective_id=0, has_side_effects=True),
@@ -403,7 +419,8 @@
         jnp.asarray(Rb), jnp.asarray(RTb), jnp.asarray(T3), jnp.asarray(TB))
     return pl.pallas_call(sum_kernel,
         out_shape=(jax.ShapeDtypeStruct((64, 4096), f32), jax.ShapeDtypeStruct((2,), f32)),
-        in_specs=[S, S, V], out_specs=(V, S), scratch_shapes=[pltpu.VMEM((66 * 32, TS), f32)],
+        in_specs=[S, S, A], out_specs=(A, S),
+        scratch_shapes=[pltpu.VMEM((128, 2, 32, TS), bf16), pltpu.VMEM((66 * 40, TS), f32), pltpu.VMEM((64, 4096), f32), D((8,)), D((8,))],
     )(first, losses, got)
 
 

time: 73.9 us -> 71.2 us (0.963)
  Pallas kernels: 73.1 us -> 70.4 us
    pallas_call x1, Pallas kernels: 68.3 us -> 65.5 us  [body(): pl.pallas_call(functools.partial(step_kernel, 8), out_shape=(jax.ShapeDty...]
where the time goes in v5:
time: 71.2 us; the launch traced here: 71 us
  Pallas kernels  70.4 us (99%)
    pallas_call x1, Pallas kernels, body(): pl.pallas_call(functools.partial(step_kernel, 8), out_shape=(jax.ShapeDty...  65.5 us
    pallas_call x1, Pallas kernels, body(): pl.pallas_call(sum_kernel, out_shape=(jax.ShapeDtypeStruct((64, 4096), f3...  4.84 us

profile of v5, /device:TPU:1, one launch (start us, length us, event | category | flops | bytes accessed | tf_op | source)
XLA Modules:
  0.0 71.0 jit_solution(15888560443494410186)
XLA Ops:
  0.6 65.5 %shard_map.104 = (bf16[128,2,32,128]{3,2,1,0:T(8,128)(2,1)}, f32[2]{0:T(128)}) custom-call(s32[4,256]{1,0:T(4,128)} %bitcast.3, f32[12]{0:T(128)} %sw.1, bf16[64,16384]{1,0:T(8,128)(2,1)} %mask_in.1, bf16[2,65536]{1,0:T(2,128)(2,1)} %target_in.1, f32[12,15,2,15]{3,2,1,0:T(2,128)} %bitcast.2, bf16[256,256]{1,0:T(8,128)(2,1)} %constant.8.clone.r_in, ...), custom_call_target="tpu_custom_call" | custom-call | tf_op jit(solution)/shard_map/pallas_call | solution.py:383
  66.2 4.8 %shard_map.105 = (f32[64,4096]{1,0:T(8,128)}, f32[2]{0:T(128)}) custom-call(s32[4,256]{1,0:T(4,128)} %bitcast.4, f32[2]{0:T(128)} %get-tuple-element.4.losses, bf16[128,2,32,128]{3,2,1,0:T(8,128)(2,1)} %get-tuple-element.5.got), custom_call_target="tpu_custom_call" | custom-call | tf_op jit(solution)/shard_map/pallas_call | solution.py:420

commit v6 on v5

--- a/solution.py
+++ b/solution.py
@@ -277,26 +277,26 @@
                 here = across.at[pl.ds(i * 8 + part * 4, 4)]
                 send(here, lines.at[pl.ds(part * 32 + pa * 8 + i * 4, 4)], gs, gr.at[i],
                     plane, at(part, (pa + j) % 4, pb, core))
-        for part in range(2):
-            pa = z if part == 0 else y
-            lines[pl.ds(part * 32 + pa * 8 + i * 4, 4)] = across[pl.ds(i * 8 + part * 4, 4)]
-
-    def to_owners(j, part):
+
+    def to_owners(j, part, begin, end):
         pa, pb = (z, y) if part == 0 else (y, z)
         b2 = (pb + j) % 4
         goal = pa * 4 + b2 if part == 0 else b2 * 4 + pa
 
         def one(n, _):
-            a_src = n // 4
+            a_src = (pa + n // 4) % 4
             x_src = n % 4
             source = x_src * 32 + at(part, a_src, pb, core)
             which = jnp.where(first[0, 2 * source + 1] >> 7 == goal, 1, 0)
-            back[part * 64 + b2 * 16 + n] = lines[part * 32 + a_src * 8 + which * 4 + x_src]
+            if begin == 0:
+                back[part * 64 + b2 * 16 + n] = across[which * 8 + part * 4 + x_src]
+            else:
+                back[part * 64 + b2 * 16 + n] = lines[part * 32 + a_src * 8 + which * 4 + x_src]
             return 0
 
-        lax.fori_loop(0, 16, one, 0, unroll=2)
-        src = back.at[pl.ds(part * 64 + b2 * 16, 16)]
-        dst = got.at[pl.ds((pb * 2 + core) * 16, 16)]
+        lax.fori_loop(begin, end, one, 0, unroll=4)
+        src = back.at[pl.ds(part * 64 + b2 * 16 + begin, end - begin)]
+        dst = got.at[pl.ds((pb * 2 + core) * 16 + begin, end - begin)]
         if j:
             send(src, dst, bs, br, plane, at(part, pa, b2, part))
         else:
@@ -325,11 +325,13 @@
     finish(1)
     to_planes(1)
     to_line(1)
-    drain(lines, 24, gr.at[0])
-    drain(lines, 24, gr.at[1])
-    for j in (2, 1, 3, 0):
-        for part in range(2):
-            to_owners(j, part)
+    for begin, end in ((0, 4), (4, 16)):
+        if begin:
+            drain(lines, 24, gr.at[0])
+            drain(lines, 24, gr.at[1])
+        for j in (2, 1, 3, 0):
+            for part in range(2):
+                to_owners(j, part, begin, end)
     drain(out, 24, s1s)
     drain(mid, 14, s2s)
     drain(grads, 12, xs)
@@ -343,13 +345,15 @@
     owner = lax.axis_index("owner")
     chip = owner // 2
     core = owner % 2
+    here = (owner >> 3) + core * (((owner >> 1) & 3) - (owner >> 3))
     loads = [pltpu.make_async_copy(got.at[pl.ds(16 * n, 16)], held.at[pl.ds(16 * n, 16)], ins.at[n]) for n in range(8)]
     for load in loads:
         load.start()
     total[...] = jnp.zeros(total.shape, f32)
 
     def step(s, _):
-        source = (s & 3) * 32 + ((s >> 2) & 3) * (8 - 6 * core) + (s >> 5) * (2 + 6 * core) + ((s >> 4) & 1)
+        line = ((s >> 2) + here) & 3
+        source = (s & 3) * 32 + line * (8 - 6 * core) + (s >> 5) * (2 + 6 * core) + ((s >> 4) & 1)
         near = first[0, 2 * source]
         far = first[0, 2 * source + 1]
         mine = jnp.where(near >> 7 == chip, near, far)
@@ -381,7 +385,7 @@
     A = pl.BlockSpec(memory_space=pl.ANY)
     D = pltpu.SemaphoreType.DMA
     got, losses = pl.pallas_call(
-        functools.partial(step_kernel, 8),
+        functools.partial(step_kernel, 24),
         out_shape=(jax.ShapeDtypeStruct((128, 2, 32, TS), bf16), jax.ShapeDtypeStruct((2,), f32)),
         in_specs=[S, S] + [A] * 7,
         out_specs=(A, S),

time: 71.2 us -> 65.3 us (0.917)
  Pallas kernels: 70.4 us -> 64.2 us
    pallas_call x1, Pallas kernels: 65.5 us -> 59.4 us  [body(): pl.pallas_call(functools.partial(step_kernel, 24), out_shape=(jax.ShapeDt...]
where the time goes in v6:
time: 65.3 us; the launch traced here: 65 us
  Pallas kernels  64.2 us (98%)
  between operations  0.8 us (1%)
    pallas_call x1, Pallas kernels, body(): pl.pallas_call(functools.partial(step_kernel, 24), out_shape=(jax.ShapeDt...  59.4 us
    pallas_call x1, Pallas kernels, body(): pl.pallas_call(sum_kernel, out_shape=(jax.ShapeDtypeStruct((64, 4096), f3...  4.87 us

profile of v6, /device:TPU:1, one launch (start us, length us, event | category | flops | bytes accessed | tf_op | source)
XLA Modules:
  0.0 65.0 jit_solution(8945972239229049029)
XLA Ops:
  0.6 59.4 %shard_map.104 = (bf16[128,2,32,128]{3,2,1,0:T(8,128)(2,1)}, f32[2]{0:T(128)}) custom-call(s32[4,256]{1,0:T(4,128)} %bitcast.3, f32[12]{0:T(128)} %sw.1, bf16[64,16384]{1,0:T(8,128)(2,1)} %mask_in.1, bf16[2,65536]{1,0:T(2,128)(2,1)} %target_in.1, f32[12,15,2,15]{3,2,1,0:T(2,128)} %bitcast.2, bf16[256,256]{1,0:T(8,128)(2,1)} %constant.8.clone.r_in, ...), custom_call_target="tpu_custom_call" | custom-call | tf_op jit(solution)/shard_map/pallas_call | solution.py:387
  60.0 4.9 %shard_map.105 = (f32[64,4096]{1,0:T(8,128)}, f32[2]{0:T(128)}) custom-call(s32[4,256]{1,0:T(4,128)} %bitcast.4, f32[2]{0:T(128)} %get-tuple-element.4.losses, bf16[128,2,32,128]{3,2,1,0:T(8,128)(2,1)} %get-tuple-element.5.got), custom_call_target="tpu_custom_call" | custom-call | tf_op jit(solution)/shard_map/pallas_call | solution.py:424

commit v7 on v6

--- a/solution.py
+++ b/solution.py
@@ -44,10 +44,11 @@
 
 
 def step_kernel(unroll, first, sw, mask_in, target_in, taps_in, r_in, rt_in, t3_in, tb_in, got, loss,
-        raw, mask, wide, target, taps, r, rt, t3, tb, rsum, out, held0, held1, held2, held3, mid, recv0, recv1, grads, across, lines, back, pad, taph, spec, sfreq, acc, field, inten, level, flow, amp,
+        raw, mask, wide, target, taps, r, rt, t3, tb, rsum, out, held0, held1, held2, held3, mid, recv0, recv1, grads, across, line1, line2, line3, back, pad, taph, spec, sfreq, acc, field, inten, level, flow, amp,
         ins, s1s, s1r, s2s, s2r, xs, xr, gs, gr, bs, br, ls):
     held = (held0, held1, held2, held3)
     recv = (recv0, recv1)
+    lines = (None, line1, line2, line3)
     plane = lax.axis_index("clip")
     owner = lax.axis_index("owner")
     me = plane * 32 + owner
@@ -271,32 +272,31 @@
 
     def to_line(i):
         drain(across, 6, xr.at[i])
-        for j in (2, 1, 3):
+        for j in (1, 3, 2):
             for part in range(2):
                 pa, pb = (z, y) if part == 0 else (y, z)
                 here = across.at[pl.ds(i * 8 + part * 4, 4)]
-                send(here, lines.at[pl.ds(part * 32 + pa * 8 + i * 4, 4)], gs, gr.at[i],
+                send(here, lines[j].at[pl.ds(part * 8 + i * 4, 4)], gs, gr.at[i * 4 + j],
                     plane, at(part, (pa + j) % 4, pb, core))
 
-    def to_owners(j, part, begin, end):
+    def to_owners(j, part, step):
         pa, pb = (z, y) if part == 0 else (y, z)
         b2 = (pb + j) % 4
         goal = pa * 4 + b2 if part == 0 else b2 * 4 + pa
 
         def one(n, _):
-            a_src = (pa + n // 4) % 4
-            x_src = n % 4
-            source = x_src * 32 + at(part, a_src, pb, core)
+            source = n * 32 + at(part, (pa - step) % 4, pb, core)
             which = jnp.where(first[0, 2 * source + 1] >> 7 == goal, 1, 0)
-            if begin == 0:
-                back[part * 64 + b2 * 16 + n] = across[which * 8 + part * 4 + x_src]
+            place = part * 64 + b2 * 16 + step * 4 + n
+            if step == 0:
+                back[place] = across[which * 8 + part * 4 + n]
             else:
-                back[part * 64 + b2 * 16 + n] = lines[part * 32 + a_src * 8 + which * 4 + x_src]
+                back[place] = lines[step][part * 8 + which * 4 + n]
             return 0
 
-        lax.fori_loop(begin, end, one, 0, unroll=4)
-        src = back.at[pl.ds(part * 64 + b2 * 16 + begin, end - begin)]
-        dst = got.at[pl.ds((pb * 2 + core) * 16 + begin, end - begin)]
+        lax.fori_loop(0, 4, one, 0, unroll=4)
+        src = back.at[pl.ds(part * 64 + b2 * 16 + step * 4, 4)]
+        dst = got.at[pl.ds((pb * 2 + core) * 16 + step * 4, 4)]
         if j:
             send(src, dst, bs, br, plane, at(part, pa, b2, part))
         else:
@@ -325,23 +325,23 @@
     finish(1)
     to_planes(1)
     to_line(1)
-    for begin, end in ((0, 4), (4, 16)):
-        if begin:
-            drain(lines, 24, gr.at[0])
-            drain(lines, 24, gr.at[1])
+    for step in (0, 1, 3, 2):
+        if step:
+            drain(lines[step], 8, gr.at[step])
+            drain(lines[step], 8, gr.at[4 + step])
         for j in (2, 1, 3, 0):
             for part in range(2):
-                to_owners(j, part, begin, end)
+                to_owners(j, part, step)
     drain(out, 24, s1s)
     drain(mid, 14, s2s)
     drain(grads, 12, xs)
-    drain(lines, 48, gs)
+    drain(back, 48, gs)
     drain(back, 112, bs)
     drain(got, 16, ls)
     drain(got, 112, br)
 
 
-def sum_kernel(first, losses, got, out, loss, held, total, rows, ins, outs):
+def sum_kernel(first, losses, got, out, loss, held, t0, t1, t2, t3, rows, ins, outs):
     owner = lax.axis_index("owner")
     chip = owner // 2
     core = owner % 2
@@ -349,26 +349,33 @@
     loads = [pltpu.make_async_copy(got.at[pl.ds(16 * n, 16)], held.at[pl.ds(16 * n, 16)], ins.at[n]) for n in range(8)]
     for load in loads:
         load.start()
-    total[...] = jnp.zeros(total.shape, f32)
-
-    def step(s, _):
-        line = ((s >> 2) + here) & 3
+    totals = (t0, t1, t2, t3)
+    for total in totals:
+        total[...] = jnp.zeros(total.shape, f32)
+
+    def add(s, odd):
+        line = (here - (s >> 2)) & 3
         source = (s & 3) * 32 + line * (8 - 6 * core) + (s >> 5) * (2 + 6 * core) + ((s >> 4) & 1)
         near = first[0, 2 * source]
         far = first[0, 2 * source + 1]
         mine = jnp.where(near >> 7 == chip, near, far)
         column = jnp.where(mine >> 7 == chip, jnp.minimum(mine & 63, 62), 64)
         for n in range(2):
-            total[pl.ds(pl.multiple_of((column + n) * 40, 8), 32), :] += held[s, n].astype(f32)
+            totals[2 * odd + n][pl.ds(pl.multiple_of((column + n) * 40, 8), 32), :] += held[s, n].astype(f32)
+
+    def step(h, _):
+        add(2 * h, 0)
+        add(2 * h + 1, 1)
         return 0
 
     for n in range(8):
         loads[n].wait()
-        lax.fori_loop(16 * n, 16 * n + 16, step, 0, unroll=4)
+        lax.fori_loop(8 * n, 8 * n + 8, step, 0, unroll=4)
     stores = []
     for t in range(8):
         for j in range(32):
-            rows[8 * t : 8 * t + 8, 128 * j : 128 * j + 128] = total[pl.ds(320 * t + j, 8, stride=40), :]
+            rows[8 * t : 8 * t + 8, 128 * j : 128 * j + 128] = sum(
+                total[pl.ds(320 * t + j, 8, stride=40), :] for total in totals)
         store = pltpu.make_async_copy(rows.at[pl.ds(8 * t, 8)], out.at[pl.ds(8 * t, 8)], outs.at[t])
         store.start()
         stores.append(store)
@@ -406,7 +413,7 @@
             *[pltpu.VMEM((8, 2, TS, TS), bf16)] * 2,
             pltpu.VMEM((16, 2, 32, TS), bf16),
             pltpu.VMEM((16, 2, 32, TS), bf16),
-            pltpu.VMEM((64, 2, 32, TS), bf16),
+            *[pltpu.VMEM((16, 2, 32, TS), bf16)] * 3,
             pltpu.VMEM((128, 2, 32, TS), bf16),
             pltpu.VMEM((CH, 16, 128), f32),
             pltpu.VMEM((CH, 48, W), bf16),
@@ -416,7 +423,7 @@
             pltpu.VMEM((CH, W, W), f32),
             pltpu.VMEM((W, W), f32),
             *[pltpu.VMEM((CH, 1, W), f32)] * 3,
-            D((10,)), D, D((4,)), D, D((2,)), D, D((2,)), D, D((2,)), D, D, D,
+            D((10,)), D, D((4,)), D, D((2,)), D, D((2,)), D, D((8,)), D, D, D,
         ],
         compiler_params=pltpu.CompilerParams(vmem_limit_bytes=56 * 2**20, collective_id=0, has_side_effects=True),
     )(first, socs_weights, mask_tiles, target, socs_kernels.transpose(1, 2, 0, 3),
@@ -424,7 +431,7 @@
     return pl.pallas_call(sum_kernel,
         out_shape=(jax.ShapeDtypeStruct((64, 4096), f32), jax.ShapeDtypeStruct((2,), f32)),
         in_specs=[S, S, A], out_specs=(A, S),
-        scratch_shapes=[pltpu.VMEM((128, 2, 32, TS), bf16), pltpu.VMEM((66 * 40, TS), f32), pltpu.VMEM((64, 4096), f32), D((8,)), D((8,))],
+        scratch_shapes=[pltpu.VMEM((128, 2, 32, TS), bf16), *[pltpu.VMEM((66 * 40, TS), f32)] * 4, pltpu.VMEM((64, 4096), f32), D((8,)), D((8,))],
     )(first, losses, got)
 
 

time: 65.3 us -> 65.9 us (level)
  no operation moved by 1% of the time
where the time goes in v7:
time: 65.9 us; the launch traced here: 65.6 us
  Pallas kernels  64.8 us (98%)
  between operations  0.8 us (1%)
    pallas_call x1, Pallas kernels, body(): pl.pallas_call(functools.partial(step_kernel, 24), out_shape=(jax.ShapeDt...  59.8 us
    pallas_call x1, Pallas kernels, body(): pl.pallas_call(sum_kernel, out_shape=(jax.ShapeDtypeStruct((64, 4096), f3...  5.02 us

profile of v7, /device:TPU:1, one launch (start us, length us, event | category | flops | bytes accessed | tf_op | source)
XLA Modules:
  0.0 65.6 jit_solution(15338175089317822472)
XLA Ops:
  0.6 59.8 %shard_map.104 = (bf16[128,2,32,128]{3,2,1,0:T(8,128)(2,1)}, f32[2]{0:T(128)}) custom-call(s32[4,256]{1,0:T(4,128)} %bitcast.3, f32[12]{0:T(128)} %sw.1, bf16[64,16384]{1,0:T(8,128)(2,1)} %mask_in.1, bf16[2,65536]{1,0:T(2,128)(2,1)} %target_in.1, f32[12,15,2,15]{3,2,1,0:T(2,128)} %bitcast.2, bf16[256,256]{1,0:T(8,128)(2,1)} %constant.8.clone.r_in, ...), custom_call_target="tpu_custom_call" | custom-call | tf_op jit(solution)/shard_map/pallas_call | solution.py:394
  60.5 5.0 %shard_map.105 = (f32[64,4096]{1,0:T(8,128)}, f32[2]{0:T(128)}) custom-call(s32[4,256]{1,0:T(4,128)} %bitcast.4, f32[2]{0:T(128)} %get-tuple-element.4.losses, bf16[128,2,32,128]{3,2,1,0:T(8,128)(2,1)} %get-tuple-element.5.got), custom_call_target="tpu_custom_call" | custom-call | tf_op jit(solution)/shard_map/pallas_call | solution.py:431

commit v8 on v6

--- a/solution.py
+++ b/solution.py
@@ -341,14 +341,11 @@
     drain(got, 112, br)
 
 
-def sum_kernel(first, losses, got, out, loss, held, total, rows, ins, outs):
+def sum_kernel(first, losses, got, out, loss, total, rows, outs):
     owner = lax.axis_index("owner")
     chip = owner // 2
     core = owner % 2
     here = (owner >> 3) + core * (((owner >> 1) & 3) - (owner >> 3))
-    loads = [pltpu.make_async_copy(got.at[pl.ds(16 * n, 16)], held.at[pl.ds(16 * n, 16)], ins.at[n]) for n in range(8)]
-    for load in loads:
-        load.start()
     total[...] = jnp.zeros(total.shape, f32)
 
     def step(s, _):
@@ -359,12 +356,10 @@
         mine = jnp.where(near >> 7 == chip, near, far)
         column = jnp.where(mine >> 7 == chip, jnp.minimum(mine & 63, 62), 64)
         for n in range(2):
-            total[pl.ds(pl.multiple_of((column + n) * 40, 8), 32), :] += held[s, n].astype(f32)
+            total[pl.ds(pl.multiple_of((column + n) * 40, 8), 32), :] += got[s, n].astype(f32)
         return 0
 
-    for n in range(8):
-        loads[n].wait()
-        lax.fori_loop(16 * n, 16 * n + 16, step, 0, unroll=4)
+    lax.fori_loop(0, 128, step, 0, unroll=16)
     stores = []
     for t in range(8):
         for j in range(32):
@@ -383,11 +378,13 @@
     Rb, RTb, T3, TB = tables()
     S = pl.BlockSpec(memory_space=pltpu.SMEM)
     A = pl.BlockSpec(memory_space=pl.ANY)
+    H = pl.BlockSpec(memory_space=pltpu.HBM)
+    V = pl.BlockSpec(memory_space=pltpu.VMEM)
     D = pltpu.SemaphoreType.DMA
     got, losses = pl.pallas_call(
         functools.partial(step_kernel, 24),
         out_shape=(jax.ShapeDtypeStruct((128, 2, 32, TS), bf16), jax.ShapeDtypeStruct((2,), f32)),
-        in_specs=[S, S] + [A] * 7,
+        in_specs=[S, S] + [H] * 7,
         out_specs=(A, S),
         scratch_shapes=[
             pltpu.VMEM((64, TS * TS), bf16),
@@ -418,13 +415,13 @@
             *[pltpu.VMEM((CH, 1, W), f32)] * 3,
             D((10,)), D, D((4,)), D, D((2,)), D, D((2,)), D, D((2,)), D, D, D,
         ],
-        compiler_params=pltpu.CompilerParams(vmem_limit_bytes=56 * 2**20, collective_id=0, has_side_effects=True),
+        compiler_params=pltpu.CompilerParams(vmem_limit_bytes=34 * 2**20, collective_id=0, has_side_effects=True),
     )(first, socs_weights, mask_tiles, target, socs_kernels.transpose(1, 2, 0, 3),
         jnp.asarray(Rb), jnp.asarray(RTb), jnp.asarray(T3), jnp.asarray(TB))
     return pl.pallas_call(sum_kernel,
         out_shape=(jax.ShapeDtypeStruct((64, 4096), f32), jax.ShapeDtypeStruct((2,), f32)),
-        in_specs=[S, S, A], out_specs=(A, S),
-        scratch_shapes=[pltpu.VMEM((128, 2, 32, TS), bf16), pltpu.VMEM((66 * 40, TS), f32), pltpu.VMEM((64, 4096), f32), D((8,)), D((8,))],
+        in_specs=[S, S, V], out_specs=(A, S),
+        scratch_shapes=[pltpu.VMEM((66 * 40, TS), f32), pltpu.VMEM((64, 4096), f32), D((8,))],
     )(first, losses, got)
 
 

time: 65.3 us -> 75.5 us (1.16)
  local copies, waits for them, and re-layouts: 0 us -> 10.2 us
    unnamed x0 -> x22, local copies, waits for them, and re-layouts: none -> 10.2 us
where the time goes in v8:
time: 75.5 us; the launch traced here: 75.1 us
  Pallas kernels  64 us (85%)
  local copies, waits for them, and re-layouts  10.2 us (14%)
  between operations  0.83 us (1%)
    pallas_call x1, Pallas kernels, body(): pl.pallas_call(functools.partial(step_kernel, 24), out_shape=(jax.ShapeDt...  59.5 us
    unnamed x22, local copies, waits for them, and re-layouts  10.2 us
    pallas_call x1, Pallas kernels, body(): pl.pallas_call(sum_kernel, out_shape=(jax.ShapeDtypeStruct((64, 4096), f3...  4.58 us

profile of v8, /device:TPU:1, one launch (start us, length us, event | category | flops | bytes accessed | tf_op | source)
XLA Modules:
  0.0 75.1 jit_solution(13829561775181737033)
XLA Ops:
  0.6 0.0 copy-start
  0.6 1.6 %copy-done = bf16[64,16384]{1,0:T(8,128)(2,1)S(1)} copy-done((bf16[64,16384]{1,0:T(8,128)(2,1)S(1)}, bf16[64,16384]{1,0:T(8,128)(2,1)}, u32[]{:S(2)}) %copy-start) | copy-done | bytes 2097176
  2.2 0.0 copy-start.2
  2.2 0.9 %copy-done.2 = bf16[2,65536]{1,0:T(2,128)(2,1)S(1)} copy-done((bf16[2,65536]{1,0:T(2,128)(2,1)S(1)}, bf16[2,65536]{1,0:T(2,128)(2,1)}, u32[]{:S(2)}) %copy-start.2) | copy-done | bytes 262168
  3.2 0.0 copy-start.3
  3.2 0.9 %copy-done.3 = f32[2,12,15,15]{3,0,2,1:T(2,128)S(1)} copy-done((f32[2,12,15,15]{3,0,2,1:T(2,128)S(1)}, f32[2,12,15,15]{3,0,2,1:T(2,128)}, u32[]{:S(2)}) %copy-start.3) | copy-done | bytes 21624
  4.1 0.0 copy-start.4
  4.1 0.9 %copy-done.4 = f32[128,256]{1,0:T(8,128)S(1)} copy-done((f32[128,256]{1,0:T(8,128)S(1)}, f32[128,256]{1,0:T(8,128)}, u32[]{:S(2)}) %copy-start.4) | copy-done | bytes 131096
  5.0 0.0 copy-start.5
  5.0 0.9 %copy-done.5 = bf16[256,256]{1,0:T(8,128)(2,1)S(1)} copy-done((bf16[256,256]{1,0:T(8,128)(2,1)S(1)}, bf16[256,256]{1,0:T(8,128)(2,1)}, u32[]{:S(2)}) %copy-start.5) | copy-done | bytes 131096
  5.9 0.0 copy-start.6
  5.9 0.9 %copy-done.6 = bf16[256,256]{1,0:T(8,128)(2,1)S(1)} copy-done((bf16[256,256]{1,0:T(8,128)(2,1)S(1)}, bf16[256,256]{1,0:T(8,128)(2,1)}, u32[]{:S(2)}) %copy-start.6) | copy-done | bytes 131096
  6.8 0.0 copy-start.7
  6.8 0.8 %copy-done.7 = bf16[256,48]{1,0:T(8,128)(2,1)S(1)} copy-done((bf16[256,48]{1,0:T(8,128)(2,1)S(1)}, bf16[256,48]{1,0:T(8,128)(2,1)}, u32[]{:S(2)}) %copy-start.7) | copy-done | bytes 24600
  7.7 0.0 copy-start.8
  7.7 0.7 copy-done.8
  8.3 0.0 copy-start.9
  8.3 0.7 copy-done.9
  9.0 59.5 %shard_map.104 = (bf16[128,2,32,128]{3,2,1,0:T(8,128)(2,1)S(1)}, f32[2]{0:T(128)S(1)}) custom-call(s32[4,256]{1,0:T(4,128)S(1)} %bitcast.4, f32[12]{0:T(128)S(1)} %copy-done.9, bf16[64,16384]{1,0:T(8,128)(2,1)S(1)} %copy-done, bf16[2,65536]{1,0:T(2,128)(2,1)S(1)} %copy-done.2, f32[12,15,2,15]{3,2,1,0:T(2,128)S(1)} %bitcast.2, ...), custom_call_target="tpu_custom_call" | custom-call | tf_op jit(solution)/shard_map/pallas_call | solution.py:384
  68.5 0.0 copy-start.1
  68.5 1.3 %copy-done.1 = bf16[128,2,32,128]{3,2,1,0:T(8,128)(2,1)} copy-done((bf16[128,2,32,128]{3,2,1,0:T(8,128)(2,1)}, bf16[128,2,32,128]{3,2,1,0:T(8,128)(2,1)S(1)}, u32[]{:S(2)}) %copy-start.1) | copy-done | bytes 2097176
  69.8 0.0 copy-start.10
  69.8 0.6 copy-done.10
  70.4 4.6 %shard_map.105 = (f32[64,4096]{1,0:T(8,128)}, f32[2]{0:T(128)}) custom-call(s32[4,256]{1,0:T(4,128)} %bitcast.3, f32[2]{0:T(128)} %copy-done.10, bf16[128,2,32,128]{3,2,1,0:T(8,128)(2,1)} %copy-done.1), custom_call_target="tpu_custom_call" | custom-call | tf_op jit(solution)/shard_map/pallas_call | solution.py:421
Async XLA Ops:
  0.6 1.6 %copy-start = (bf16[64,16384]{1,0:T(8,128)(2,1)S(1)}, bf16[64,16384]{1,0:T(8,128)(2,1)}, u32[]{:S(2)}) copy-start(bf16[64,16384]{1,0:T(8,128)(2,1)} %mask_in.1) | copy-start | bytes 6291460
  2.2 0.9 %copy-start.2 = (bf16[2,65536]{1,0:T(2,128)(2,1)S(1)}, bf16[2,65536]{1,0:T(2,128)(2,1)}, u32[]{:S(2)}) copy-start(bf16[2,65536]{1,0:T(2,128)(2,1)} %target_in.1) | copy-start | bytes 786436
  3.2 0.9 %copy-start.3 = (f32[2,12,15,15]{3,0,2,1:T(2,128)S(1)}, f32[2,12,15,15]{3,0,2,1:T(2,128)}, u32[]{:S(2)}) copy-start(f32[2,12,15,15]{3,0,2,1:T(2,128)} %param.12) | copy-start | bytes 64804
  4.1 0.9 %copy-start.4 = (f32[128,256]{1,0:T(8,128)S(1)}, f32[128,256]{1,0:T(8,128)}, u32[]{:S(2)}) copy-start(f32[128,256]{1,0:T(8,128)} %constant.11.clone.tb_in) | copy-start | bytes 393220
  5.0 0.9 %copy-start.5 = (bf16[256,256]{1,0:T(8,128)(2,1)S(1)}, bf16[256,256]{1,0:T(8,128)(2,1)}, u32[]{:S(2)}) copy-start(bf16[256,256]{1,0:T(8,128)(2,1)} %constant.9.clone.rt_in) | copy-start | bytes 393220
  5.9 0.9 %copy-start.6 = (bf16[256,256]{1,0:T(8,128)(2,1)S(1)}, bf16[256,256]{1,0:T(8,128)(2,1)}, u32[]{:S(2)}) copy-start(bf16[256,256]{1,0:T(8,128)(2,1)} %constant.8.clone.r_in) | copy-start | bytes 393220
  6.8 0.8 %copy-start.7 = (bf16[256,48]{1,0:T(8,128)(2,1)S(1)}, bf16[256,48]{1,0:T(8,128)(2,1)}, u32[]{:S(2)}) copy-start(bf16[256,48]{1,0:T(8,128)(2,1)} %constant.10.clone.t3_in) | copy-start | bytes 73732
  7.7 0.7 copy-start.8
  8.3 0.7 copy-start.9
  68.5 1.3 %copy-start.1 = (bf16[128,2,32,128]{3,2,1,0:T(8,128)(2,1)}, bf16[128,2,32,128]{3,2,1,0:T(8,128)(2,1)S(1)}, u32[]{:S(2)}) copy-start(bf16[128,2,32,128]{3,2,1,0:T(8,128)(2,1)S(1)} %get-tuple-element.5.got) | copy-start | bytes 6291460
  69.8 0.6 copy-start.10

commit v9 on v7

--- a/solution.py
+++ b/solution.py
@@ -75,6 +75,10 @@
         for c in range(2):
             partners.append((plane, at(0, (z + j) % 4, y, c)))
             partners.append((plane, at(0, z, (y + j) % 4, c)))
+    for j in (1, 2, 3):
+        for p in (1, 2, 3):
+            partners.append(((plane + p) % 4, at(0, (z + j) % 4, y, core)))
+            partners.append(((plane + p) % 4, at(0, z, (y + j) % 4, core)))
     for to in partners:
         pl.semaphore_signal(barrier, inc=1, device_id=to, device_id_type=MESH)
 
@@ -279,6 +283,22 @@
                 send(here, lines[j].at[pl.ds(part * 8 + i * 4, 4)], gs, gr.at[i * 4 + j],
                     plane, at(part, (pa + j) % 4, pb, core))
 
+    def to_planes_and_line(i):
+        for j in (0, 1, 3, 2):
+            for q in (1, 3, 2, 0):
+                p = (plane + q) % 4
+                for part in range(2):
+                    pa, pb = (z, y) if part == 0 else (y, z)
+                    src = grads.at[i * 8 + p * 2 + part]
+                    if j:
+                        send(src, lines[j].at[part * 8 + i * 4 + plane], gs, gr.at[i * 4 + j],
+                            p, at(part, (pa + j) % 4, pb, core))
+                    elif q:
+                        send(src, across.at[i * 8 + part * 4 + plane], xs, xr.at[i], p, owner)
+        for part in range(2):
+            across[i * 8 + part * 4 + plane] = grads[i * 8 + plane * 2 + part]
+        drain(across, 6, xr.at[i])
+
     def to_owners(j, part, step):
         pa, pb = (z, y) if part == 0 else (y, z)
         b2 = (pb + j) % 4
@@ -323,8 +343,7 @@
     resist(1)
     backward()
     finish(1)
-    to_planes(1)
-    to_line(1)
+    to_planes_and_line(1)
     for step in (0, 1, 3, 2):
         if step:
             drain(lines[step], 8, gr.at[step])
@@ -341,7 +360,7 @@
     drain(got, 112, br)
 
 
-def sum_kernel(first, losses, got, out, loss, held, t0, t1, t2, t3, rows, ins, outs):
+def sum_kernel(first, losses, got, out, loss, held, total, rows, ins, outs):
     owner = lax.axis_index("owner")
     chip = owner // 2
     core = owner % 2
@@ -349,11 +368,9 @@
     loads = [pltpu.make_async_copy(got.at[pl.ds(16 * n, 16)], held.at[pl.ds(16 * n, 16)], ins.at[n]) for n in range(8)]
     for load in loads:
         load.start()
-    totals = (t0, t1, t2, t3)
-    for total in totals:
-        total[...] = jnp.zeros(total.shape, f32)
-
-    def add(s, odd):
+    total[...] = jnp.zeros(total.shape, f32)
+
+    def step(s, _):
         line = (here - (s >> 2)) & 3
         source = (s & 3) * 32 + line * (8 - 6 * core) + (s >> 5) * (2 + 6 * core) + ((s >> 4) & 1)
         near = first[0, 2 * source]
@@ -361,21 +378,16 @@
         mine = jnp.where(near >> 7 == chip, near, far)
         column = jnp.where(mine >> 7 == chip, jnp.minimum(mine & 63, 62), 64)
         for n in range(2):
-            totals[2 * odd + n][pl.ds(pl.multiple_of((column + n) * 40, 8), 32), :] += held[s, n].astype(f32)
-
-    def step(h, _):
-        add(2 * h, 0)
-        add(2 * h + 1, 1)
+            total[pl.ds(pl.multiple_of((column + n) * 40, 8), 32), :] += held[s, n].astype(f32)
         return 0
 
     for n in range(8):
         loads[n].wait()
-        lax.fori_loop(8 * n, 8 * n + 8, step, 0, unroll=4)
+        lax.fori_loop(16 * n, 16 * n + 16, step, 0, unroll=16)
     stores = []
     for t in range(8):
         for j in range(32):
-            rows[8 * t : 8 * t + 8, 128 * j : 128 * j + 128] = sum(
-                total[pl.ds(320 * t + j, 8, stride=40), :] for total in totals)
+            rows[8 * t : 8 * t + 8, 128 * j : 128 * j + 128] = total[pl.ds(320 * t + j, 8, stride=40), :]
         store = pltpu.make_async_copy(rows.at[pl.ds(8 * t, 8)], out.at[pl.ds(8 * t, 8)], outs.at[t])
         store.start()
         stores.append(store)
@@ -431,7 +443,7 @@
     return pl.pallas_call(sum_kernel,
         out_shape=(jax.ShapeDtypeStruct((64, 4096), f32), jax.ShapeDtypeStruct((2,), f32)),
         in_specs=[S, S, A], out_specs=(A, S),
-        scratch_shapes=[pltpu.VMEM((128, 2, 32, TS), bf16), *[pltpu.VMEM((66 * 40, TS), f32)] * 4, pltpu.VMEM((64, 4096), f32), D((8,)), D((8,))],
+        scratch_shapes=[pltpu.VMEM((128, 2, 32, TS), bf16), pltpu.VMEM((66 * 40, TS), f32), pltpu.VMEM((64, 4096), f32), D((8,)), D((8,))],
     )(first, losses, got)
 
 

time: 65.9 us -> 64.1 us (0.973)
  Pallas kernels: 64.8 us -> 63.1 us
    pallas_call x1, Pallas kernels: 59.8 us -> 58.9 us  [body(): pl.pallas_call(functools.partial(step_kernel, 24), out_shape=(jax.ShapeDt...]
    pallas_call x1, Pallas kernels: 5.02 us -> 4.27 us  [body(): pl.pallas_call(sum_kernel, out_shape=(jax.ShapeDtypeStruct((64, 4096), f3...]
where the time goes in v9:
time: 64.1 us; the launch traced here: 63.9 us
  Pallas kernels  63.1 us (98%)
  between operations  0.8 us (1%)
    pallas_call x1, Pallas kernels, body(): pl.pallas_call(functools.partial(step_kernel, 24), out_shape=(jax.ShapeDt...  58.9 us
    pallas_call x1, Pallas kernels, body(): pl.pallas_call(sum_kernel, out_shape=(jax.ShapeDtypeStruct((64, 4096), f3...  4.27 us

profile of v9, /device:TPU:1, one launch (start us, length us, event | category | flops | bytes accessed | tf_op | source)
XLA Modules:
  0.0 63.9 jit_solution(3143167615178026956)
XLA Ops:
  0.6 58.9 %shard_map.104 = (bf16[128,2,32,128]{3,2,1,0:T(8,128)(2,1)}, f32[2]{0:T(128)}) custom-call(s32[4,256]{1,0:T(4,128)} %bitcast.3, f32[12]{0:T(128)} %sw.1, bf16[64,16384]{1,0:T(8,128)(2,1)} %mask_in.1, bf16[2,65536]{1,0:T(2,128)(2,1)} %target_in.1, f32[12,15,2,15]{3,2,1,0:T(2,128)} %bitcast.2, bf16[256,256]{1,0:T(8,128)(2,1)} %constant.8.clone.r_in, ...), custom_call_target="tpu_custom_call" | custom-call | tf_op jit(solution)/shard_map/pallas_call | solution.py:406
  59.5 4.3 %shard_map.105 = (f32[64,4096]{1,0:T(8,128)}, f32[2]{0:T(128)}) custom-call(s32[4,256]{1,0:T(4,128)} %bitcast.4, f32[2]{0:T(128)} %get-tuple-element.4.losses, bf16[128,2,32,128]{3,2,1,0:T(8,128)(2,1)} %get-tuple-element.5.got), custom_call_target="tpu_custom_call" | custom-call | tf_op jit(solution)/shard_map/pallas_call | solution.py:443

commit v10 on v9

--- a/solution.py
+++ b/solution.py
@@ -68,6 +68,14 @@
         pltpu.make_async_remote_copy(src_ref=src, dst_ref=dst, send_sem=send_sem, recv_sem=recv_sem,
             device_id=(p, to), device_id_type=MESH).start()
 
+    loads = [pltpu.make_async_copy(mask_in.at[pl.ds(16 * n, 16)], raw.at[pl.ds(16 * n, 16)], ins.at[n]) for n in range(4)]
+    loads += [
+        pltpu.make_async_copy(src, dst, ins.at[4 + n])
+        for n, (src, dst) in enumerate(((taps_in, taps), (tb_in, tb), (t3_in, t3), (target_in, wide), (r_in, r), (rt_in, rt)))
+    ]
+    for load in loads:
+        load.start()
+
     barrier = pltpu.get_barrier_semaphore()
     partners = [(plane, owner + 1 - 2 * core)]
     for j in (1, 2, 3):
@@ -81,14 +89,6 @@
             partners.append(((plane + p) % 4, at(0, z, (y + j) % 4, core)))
     for to in partners:
         pl.semaphore_signal(barrier, inc=1, device_id=to, device_id_type=MESH)
-
-    loads = [pltpu.make_async_copy(mask_in.at[pl.ds(16 * n, 16)], raw.at[pl.ds(16 * n, 16)], ins.at[n]) for n in range(4)]
-    loads += [
-        pltpu.make_async_copy(src, dst, ins.at[4 + n])
-        for n, (src, dst) in enumerate(((taps_in, taps), (tb_in, tb), (t3_in, t3), (target_in, wide), (r_in, r), (rt_in, rt)))
-    ]
-    for load in loads:
-        load.start()
 
     a = z + core * (y - z)
     b = y + core * (z - y)
@@ -149,7 +149,7 @@
             flat[pl.ds((16 * n + 8) * PITCH + j, 8, stride=PITCH), :] = v[8:]
             return 0
 
-        lax.fori_loop(0, TS, rows, 0, unroll=8)
+        lax.fori_loop(0, TS, rows, 0, unroll=32)
 
     pick(0)
     pl.semaphore_wait(barrier, len(partners))
@@ -207,24 +207,24 @@
         rounded = sums.astype(bf16).astype(f32)
         t = (dot(r[...], x) - rsum[...] * (0.5 - (rounded - sums) * (1.0 / W))).astype(bf16)
         zero = flow[...] * jnp.sum(rounded)
-        level[...] = amp[...] * (0.5 * flow[...] + (zero.astype(bf16).astype(f32) - zero) * (1.0 / (W * W)))
+        level[CH * i : CH * i + CH] = amp[...] * (0.5 * flow[...] + (zero.astype(bf16).astype(f32) - zero) * (1.0 / (W * W)))
         cc, cs, sc, ss = quarters(dot(t, rt[...]) * (0.5 / (HF * HF)))
-        sfreq[0] = cc - ss
-        sfreq[1] = sc + cs
-        sfreq[2] = cc + ss
-        sfreq[3] = sc - cs
+        sfreq[4 * i] = cc - ss
+        sfreq[4 * i + 1] = sc + cs
+        sfreq[4 * i + 2] = cc + ss
+        sfreq[4 * i + 3] = sc - cs
 
     def back_to_pixels(aa, bb, a2, b2):
         u = dot(whole(aa + a2, bb - b2, bb + b2, a2 - aa).astype(bf16), r[...]).astype(bf16)
         return dot(rt[...], u)
 
-    def forward():
+    def forward(i):
         inten[...] = jnp.zeros((W, W), f32)
 
         def channel(c, _):
-            p, q, p2, q2 = (sfreq[j] for j in range(4))
+            p, q, p2, q2 = (sfreq[4 * i + j] for j in range(4))
             m, n, m2, n2 = (spec[c, j] for j in range(4))
-            e = back_to_pixels(p * m - q * n, p * n + q * m, p2 * m2 - q2 * n2, p2 * n2 + q2 * m2) + level[c]
+            e = back_to_pixels(p * m - q * n, p * n + q * m, p2 * m2 - q2 * n2, p2 * n2 + q2 * m2) + level[CH * i + c]
             field[c] = e
             inten[...] = inten[...] + e * e
             return 0
@@ -331,14 +331,14 @@
 
     drain(recv[0], 7, s2r.at[0])
     transform(0)
-    forward()
+    forward(0)
     resist(0)
+    drain(recv[1], 7, s2r.at[1])
+    transform(1)
     backward()
     finish(0)
     to_planes(0)
-    drain(recv[1], 7, s2r.at[1])
-    transform(1)
-    forward()
+    forward(1)
     to_line(0)
     resist(1)
     backward()
@@ -430,11 +430,12 @@
             pltpu.VMEM((CH, 16, 128), f32),
             pltpu.VMEM((CH, 48, W), bf16),
             pltpu.VMEM((CH, 4, HF, HF), f32),
-            pltpu.VMEM((4, HF, HF), f32),
+            pltpu.VMEM((8, HF, HF), f32),
             pltpu.VMEM((4, HF, HF), f32),
             pltpu.VMEM((CH, W, W), f32),
             pltpu.VMEM((W, W), f32),
-            *[pltpu.VMEM((CH, 1, W), f32)] * 3,
+            pltpu.VMEM((2 * CH, 1, W), f32),
+            *[pltpu.VMEM((CH, 1, W), f32)] * 2,
             D((10,)), D, D((4,)), D, D((2,)), D, D((2,)), D, D((8,)), D, D, D,
         ],
         compiler_params=pltpu.CompilerParams(vmem_limit_bytes=56 * 2**20, collective_id=0, has_side_effects=True),

time: 64.1 us -> 66.8 us (1.042)
  Pallas kernels: 63.1 us -> 65.8 us
    pallas_call x1, Pallas kernels: 58.9 us -> 61.5 us  [body(): pl.pallas_call(functools.partial(step_kernel, 24), out_shape=(jax.ShapeDt...]
where the time goes in v10:
time: 66.8 us; the launch traced here: 66.6 us
  Pallas kernels  65.8 us (99%)
  between operations  0.8 us (1%)
    pallas_call x1, Pallas kernels, body(): pl.pallas_call(functools.partial(step_kernel, 24), out_shape=(jax.ShapeDt...  61.5 us
    pallas_call x1, Pallas kernels, body(): pl.pallas_call(sum_kernel, out_shape=(jax.ShapeDtypeStruct((64, 4096), f3...  4.28 us

profile of v10, /device:TPU:1, one launch (start us, length us, event | category | flops | bytes accessed | tf_op | source)
XLA Modules:
  0.0 66.6 jit_solution(5584702279087395215)
XLA Ops:
  0.6 61.5 %shard_map.104 = (bf16[128,2,32,128]{3,2,1,0:T(8,128)(2,1)}, f32[2]{0:T(128)}) custom-call(s32[4,256]{1,0:T(4,128)} %bitcast.3, f32[12]{0:T(128)} %sw.1, bf16[64,16384]{1,0:T(8,128)(2,1)} %mask_in.1, bf16[2,65536]{1,0:T(2,128)(2,1)} %target_in.1, f32[12,15,2,15]{3,2,1,0:T(2,128)} %bitcast.2, bf16[256,256]{1,0:T(8,128)(2,1)} %constant.8.clone.r_in, ...), custom_call_target="tpu_custom_call" | custom-call | tf_op jit(solution)/shard_map/pallas_call | solution.py:406
  62.1 4.3 %shard_map.105 = (f32[64,4096]{1,0:T(8,128)}, f32[2]{0:T(128)}) custom-call(s32[4,256]{1,0:T(4,128)} %bitcast.4, f32[2]{0:T(128)} %get-tuple-element.4.losses, bf16[128,2,32,128]{3,2,1,0:T(8,128)(2,1)} %get-tuple-element.5.got), custom_call_target="tpu_custom_call" | custom-call | tf_op jit(solution)/shard_map/pallas_call | solution.py:444

commit v11 on v9

--- a/solution.py
+++ b/solution.py
@@ -68,6 +68,14 @@
         pltpu.make_async_remote_copy(src_ref=src, dst_ref=dst, send_sem=send_sem, recv_sem=recv_sem,
             device_id=(p, to), device_id_type=MESH).start()
 
+    loads = [pltpu.make_async_copy(mask_in.at[pl.ds(16 * n, 16)], raw.at[pl.ds(16 * n, 16)], ins.at[n]) for n in range(4)]
+    loads += [
+        pltpu.make_async_copy(src, dst, ins.at[4 + n])
+        for n, (src, dst) in enumerate(((taps_in, taps), (tb_in, tb), (t3_in, t3), (target_in, wide), (r_in, r), (rt_in, rt)))
+    ]
+    for load in loads:
+        load.start()
+
     barrier = pltpu.get_barrier_semaphore()
     partners = [(plane, owner + 1 - 2 * core)]
     for j in (1, 2, 3):
@@ -81,14 +89,6 @@
             partners.append(((plane + p) % 4, at(0, z, (y + j) % 4, core)))
     for to in partners:
         pl.semaphore_signal(barrier, inc=1, device_id=to, device_id_type=MESH)
-
-    loads = [pltpu.make_async_copy(mask_in.at[pl.ds(16 * n, 16)], raw.at[pl.ds(16 * n, 16)], ins.at[n]) for n in range(4)]
-    loads += [
-        pltpu.make_async_copy(src, dst, ins.at[4 + n])
-        for n, (src, dst) in enumerate(((taps_in, taps), (tb_in, tb), (t3_in, t3), (target_in, wide), (r_in, r), (rt_in, rt)))
-    ]
-    for load in loads:
-        load.start()
 
     a = z + core * (y - z)
     b = y + core * (z - y)

time: 64.1 us -> 64.1 us (level)
  no operation moved by 1% of the time
where the time goes in v11:
time: 64.1 us; the launch traced here: 63.9 us
  Pallas kernels  63.1 us (98%)
  between operations  0.8 us (1%)
    pallas_call x1, Pallas kernels, body(): pl.pallas_call(functools.partial(step_kernel, 24), out_shape=(jax.ShapeDt...  58.9 us
    pallas_call x1, Pallas kernels, body(): pl.pallas_call(sum_kernel, out_shape=(jax.ShapeDtypeStruct((64, 4096), f3...  4.27 us

profile of v11, /device:TPU:1, one launch (start us, length us, event | category | flops | bytes accessed | tf_op | source)
XLA Modules:
  0.0 63.9 jit_solution(6375076360595453041)
XLA Ops:
  0.6 58.9 %shard_map.104 = (bf16[128,2,32,128]{3,2,1,0:T(8,128)(2,1)}, f32[2]{0:T(128)}) custom-call(s32[4,256]{1,0:T(4,128)} %bitcast.3, f32[12]{0:T(128)} %sw.1, bf16[64,16384]{1,0:T(8,128)(2,1)} %mask_in.1, bf16[2,65536]{1,0:T(2,128)(2,1)} %target_in.1, f32[12,15,2,15]{3,2,1,0:T(2,128)} %bitcast.2, bf16[256,256]{1,0:T(8,128)(2,1)} %constant.8.clone.r_in, ...), custom_call_target="tpu_custom_call" | custom-call | tf_op jit(solution)/shard_map/pallas_call | solution.py:406
  59.5 4.3 %shard_map.105 = (f32[64,4096]{1,0:T(8,128)}, f32[2]{0:T(128)}) custom-call(s32[4,256]{1,0:T(4,128)} %bitcast.4, f32[2]{0:T(128)} %get-tuple-element.4.losses, bf16[128,2,32,128]{3,2,1,0:T(8,128)(2,1)} %get-tuple-element.5.got), custom_call_target="tpu_custom_call" | custom-call | tf_op jit(solution)/shard_map/pallas_call | solution.py:443
